TPU v7x, 128 devices: a whole 4x4x4 slice. The times are simulated.
128 devices in a mesh: section: 2 (over x_hi), ctx: 16 (over x_lo, z, core), fsdp: 4 (over y).
Axes of the slice: x: 4 (x_hi: 2, x_lo: 2; x = x_hi * 2 + x_lo), y: 4, z: 4, core: 2. Of those that a mesh axis runs over, the one named last changes fastest.
Arguments:
- inputs: bfloat16 [2, 4, 2048, 768], P(None, 'fsdp', 'ctx'), may hold values from -6 to 6
- out_grad: bfloat16 [2, 4, 2048, 768], P(None, 'fsdp', 'ctx'), may hold values from -6 to 6
- doc_lengths: int32 [2, 4, 4], P(None, 'fsdp'), may hold values from 0 to 2048, as said below
- attn_gain: bfloat16 [2, 768], P('section', 'fsdp'), may hold values from 0.099609375 to 1.8984375
- qkv_weight: bfloat16 [2, 768, 2304], P('section', 'fsdp'), may hold values from -0.21875 to 0.21875
- proj_weight: bfloat16 [2, 768, 768], P('section', 'fsdp'), may hold values from -1.25 to 1.25
- mlp_gain: bfloat16 [2, 768], P('section', 'fsdp'), may hold values from 0.099609375 to 1.8984375
- lift_weight: bfloat16 [2, 768, 2304], P('section', 'fsdp'), may hold values from -0.21875 to 0.21875
- down_weight: bfloat16 [2, 1152, 768], P('section', 'fsdp'), may hold values from -0.1875 to 0.1875
Outputs:
- acts: bfloat16 [2, 2, 4, 2048, 768], P('section', None, 'fsdp', 'ctx')
- in_grads: bfloat16 [2, 2, 4, 2048, 768], P('section', None, 'fsdp', 'ctx')
- attn_gain_grad: float32 [2, 768], P('section', 'fsdp')
- qkv_grad: float32 [2, 768, 2304], P('section', 'fsdp')
- proj_grad: float32 [2, 768, 768], P('section', 'fsdp')
- mlp_gain_grad: float32 [2, 768], P('section', 'fsdp')
- lift_grad: float32 [2, 768, 2304], P('section', 'fsdp')
- down_grad: float32 [2, 1152, 768], P('section', 'fsdp')
Inputs may be any that keep to these rules, and one draw needn't show every extreme that they name: `doc_lengths`: each sequence's 4 document lengths sum to 2048; some may be zero; one sequence, chosen at random, is a single document.
All inputs are finite; a program needn't handle non-finite values.
Results may differ from a plain program's by a relative error of at most 0.035.
Values may be sent and summed in bfloat16 or wider, within the bound.
No kernel may reach another device: no remote copies, remote signals or barrier semaphores. Data moves between devices by JAX's collectives and lax.ppermute only.
A program may use at most 128 MiB of HBM per device.

v0:
```python
import math

import jax
import jax.numpy as jnp
from jax import lax
from jax.sharding import PartitionSpec as P

D = 768
HD = 64
HALF = 64
SEQ_LEN = 2048


norm_eps = 1e-05
rope_base = 10000.0
masked_score = -1e30
root_half = 0.7071067811865476
inv_root_tau = 0.3989422804014327


def with_halo_2(block, sides, width):
    for axis, dim in sides:
        count = lax.axis_size(axis)
        forward = [(i, i + 1) for i in range(count - 1)]
        backward = [(target, source) for source, target in forward]
        low = lax.ppermute(
            lax.slice_in_dim(block, block.shape[dim] - width, None, axis=dim), axis, forward
        )
        high = lax.ppermute(lax.slice_in_dim(block, 0, width, axis=dim), axis, backward)
        block = jnp.concatenate([low, block, high], axis=dim)
    return block


def shifted(block, axis, distance):
    devices = range(lax.axis_size(axis))
    route = [(i - distance, i) for i in devices if i - distance in devices]
    return lax.ppermute(block, axis, route)


def layer_norm(hidden, gain):
    centre = hidden - jnp.mean(hidden, axis=-1, keepdims=True)
    inv_scale = lax.rsqrt(jnp.mean(centre * centre, axis=-1, keepdims=True) + norm_eps)
    normed = centre * inv_scale
    return (normed * gain, normed, inv_scale)


def norm_back(grad_out, gain, normed, inv_scale):
    grad_normed = grad_out * gain
    gain_grad = jnp.sum(grad_out * normed, axis=0)
    inner = (
        grad_normed
        - jnp.mean(grad_normed, axis=-1, keepdims=True)
        - normed * jnp.mean(grad_normed * normed, axis=-1, keepdims=True)
    )
    return (inner * inv_scale, gain_grad)


def rope_tables(positions):
    half_dim = HD // 2
    frequencies = rope_base ** (-(jnp.arange(half_dim, dtype=jnp.float32) * 2.0) / HD)
    angles = positions.astype(jnp.float32)[:, None] * frequencies[None, :]
    angles = jnp.concatenate([angles, angles], axis=1)
    return (jnp.cos(angles)[:, None, :], jnp.sin(angles)[:, None, :])


def rotate(values_in, cosine_table, sine_table, turn_sign):
    half_dim = values_in.shape[-1] // 2
    turned = jnp.concatenate([-values_in[..., half_dim:], values_in[..., :half_dim]], axis=-1)
    return values_in * cosine_table + turn_sign * (turned * sine_table)


def doc_numbers(positions, lengths):
    doc_ends = jnp.cumsum(lengths)
    return jnp.sum((positions[:, None] >= doc_ends[None, :]).astype(jnp.int32), axis=1)


def key_mask(query_pos, key_pos, lengths):
    within = jnp.abs(query_pos[:, None] - key_pos[None, :]) <= HALF
    inside = (key_pos >= 0) & (key_pos < SEQ_LEN)
    same_doc = doc_numbers(query_pos, lengths)[:, None] == doc_numbers(key_pos, lengths)[None, :]
    return within & inside[None, :] & same_doc


def outer_sum(left, right):
    return lax.dot_general(
        left, right, (((0,), (0,)), ((), ())), preferred_element_type=jnp.float32
    )


def back_dot(grad_in, weight):
    return lax.dot_general(
        grad_in, weight, (((1,), (1,)), ((), ())), preferred_element_type=jnp.float32
    )


def block_scores(queries, with_halo, block_index, block_rows, offset, lengths):
    row_count, head_count, head_size = queries.shape
    key_span = block_rows + 2 * HALF
    row_start = block_index * block_rows
    key_blk = with_halo[:, 0].reshape(key_span, head_count, head_size)
    value_blk = with_halo[:, 1].reshape(key_span, head_count, head_size)
    query_pos = offset + row_start + jnp.arange(block_rows, dtype=jnp.int32)
    key_pos = offset + row_start - HALF + jnp.arange(key_span, dtype=jnp.int32)
    allowed = key_mask(query_pos, key_pos, lengths)
    scores = jnp.einsum("ihd,jhd->hij", queries, key_blk, preferred_element_type=jnp.float32) * (
        1.0 / math.sqrt(head_size)
    )
    scores = jnp.where(allowed[None], scores, masked_score)
    return (scores, queries, key_blk, value_blk, row_start)


def attend_forward(queries, with_halo, offset, lengths):
    row_count, head_count, head_size = queries.shape
    block_rows = min(row_count, 512)

    def one_block(block_index):
        scores, query_blk, key_blk, value_blk, row_start = block_scores(
            queries, with_halo, block_index, block_rows, offset, lengths
        )
        row_peak = jnp.max(scores, axis=-1, keepdims=True)
        expo_terms = jnp.exp(scores - row_peak)
        row_total = jnp.sum(expo_terms, axis=-1, keepdims=True)
        attn_probs = (expo_terms / row_total).astype(jnp.bfloat16)
        attended = jnp.einsum(
            "hij,jhd->ihd", attn_probs, value_blk, preferred_element_type=jnp.float32
        )
        return (
            attended.reshape(block_rows, head_count * head_size),
            (row_peak + jnp.log(row_total))[..., 0],
        )

    attended, log_totals = lax.map(one_block, jnp.arange(row_count // block_rows, dtype=jnp.int32))
    return (attended.reshape(row_count, head_count * head_size), log_totals)


def attend_backward(queries, with_halo, log_totals, grad_attended, offset, lengths):
    row_count, head_count, head_size = queries.shape
    block_rows = min(row_count, 512)
    key_span = block_rows + 2 * HALF
    score_scale = 1.0 / math.sqrt(head_size)

    def one_block(block_index, state_pair):
        grad_query, grad_wide = state_pair
        scores, query_blk, key_blk, value_blk, row_start = block_scores(
            queries, with_halo, block_index, block_rows, offset, lengths
        )
        attn_probs = jnp.exp(scores - log_totals[block_index][..., None])
        grad_blk = grad_attended.reshape(block_rows, head_count, head_size)
        grad_probs = jnp.einsum(
            "ihd,jhd->hij", grad_blk, value_blk, preferred_element_type=jnp.float32
        )
        row_inner = jnp.sum(attn_probs * grad_probs, axis=-1, keepdims=True)
        grad_scores = (attn_probs * (grad_probs - row_inner)).astype(jnp.bfloat16)
        query_part = (
            jnp.einsum("hij,jhd->ihd", grad_scores, key_blk, preferred_element_type=jnp.float32)
            * score_scale
        )
        key_part = (
            jnp.einsum("hij,ihd->jhd", grad_scores, query_blk, preferred_element_type=jnp.float32)
            * score_scale
        )
        value_part = jnp.einsum(
            "hij,ihd->jhd",
            attn_probs.astype(jnp.bfloat16),
            grad_blk,
            preferred_element_type=jnp.float32,
        )
        grad_query = query_part
        current = grad_wide
        update = jnp.stack(
            [
                key_part.reshape(key_span, head_count * head_size),
                value_part.reshape(key_span, head_count * head_size),
            ],
            axis=1,
        )
        grad_wide = current + update
        return (grad_query, grad_wide)

    initial = (
        jnp.zeros((row_count, head_count, head_size), jnp.float32),
        jnp.zeros((row_count + 2 * HALF, 2, head_count * head_size), jnp.float32),
    )
    return lax.fori_loop(0, row_count // block_rows, one_block, initial)


def forward_layer(hidden, weights, lengths, offset):
    attn_gain, qkv_weight, proj_weight, mlp_gain, lift_weight, down_weight = weights
    row_count = hidden.shape[0]
    head_count = D // HD
    inner_width = down_weight.shape[0]
    attn_input, normed_one, scale_one = layer_norm(hidden, attn_gain.astype(jnp.float32))
    attn_input = attn_input.astype(jnp.bfloat16)
    packed = jnp.dot(attn_input, qkv_weight, preferred_element_type=jnp.float32)
    cosine_table, sine_table = rope_tables(offset + jnp.arange(row_count, dtype=jnp.int32))
    queries = rotate(
        packed[:, :D].reshape(row_count, head_count, HD), cosine_table, sine_table, 1.0
    ).astype(jnp.bfloat16)
    key_rot = rotate(
        packed[:, D : 2 * D].reshape(row_count, head_count, HD), cosine_table, sine_table, 1.0
    ).astype(jnp.bfloat16)
    key_value = jnp.stack(
        [key_rot.reshape(row_count, D), packed[:, 2 * D :].astype(jnp.bfloat16)], axis=1
    )
    with_halo = with_halo_2(key_value, (("ctx", 0),), HALF)
    attended, log_totals = attend_forward(queries, with_halo, offset, lengths)
    attended_low = attended.astype(jnp.bfloat16)
    mixed_sum = hidden + jnp.dot(attended_low, proj_weight, preferred_element_type=jnp.float32)
    mlp_input, normed_two, scale_two = layer_norm(mixed_sum, mlp_gain.astype(jnp.float32))
    mlp_input = mlp_input.astype(jnp.bfloat16)
    lifted = jnp.dot(mlp_input, lift_weight, preferred_element_type=jnp.float32)
    active_low = (
        jax.nn.gelu(lifted[:, :inner_width], approximate=False) * lifted[:, inner_width:]
    ).astype(jnp.bfloat16)
    result = mixed_sum + jnp.dot(active_low, down_weight, preferred_element_type=jnp.float32)
    saved_state = (
        normed_one,
        scale_one,
        attn_input,
        queries,
        with_halo,
        log_totals,
        attended_low,
        normed_two,
        scale_two,
        mlp_input,
        lifted,
        active_low,
    )
    return (result.astype(jnp.bfloat16), saved_state)


def backward_layer(grad_out, saved_state, weights, lengths, offset):
    attn_gain, qkv_weight, proj_weight, mlp_gain, lift_weight, down_weight = weights
    (
        normed_one,
        scale_one,
        attn_input,
        queries,
        with_halo,
        log_totals,
        attended_low,
        normed_two,
        scale_two,
        mlp_input,
        lifted,
        active_low,
    ) = saved_state
    row_count = grad_out.shape[0]
    head_count = D // HD
    inner_width = down_weight.shape[0]
    grad_low = grad_out.astype(jnp.bfloat16)
    down_term = outer_sum(active_low, grad_low)
    grad_active = back_dot(grad_low, down_weight)
    gate_part = lifted[:, :inner_width]
    up_part = lifted[:, inner_width:]
    gate_cdf = 0.5 * (1.0 + lax.erf(gate_part * root_half))
    gate_pdf = jnp.exp(-0.5 * gate_part * gate_part) * inv_root_tau
    grad_lifted = jnp.concatenate(
        [
            grad_active * up_part * (gate_cdf + gate_part * gate_pdf),
            grad_active * jax.nn.gelu(gate_part, approximate=False),
        ],
        axis=1,
    ).astype(jnp.bfloat16)
    lift_term = outer_sum(mlp_input, grad_lifted)
    grad_mlp_norm, mlp_gain_term = norm_back(
        back_dot(grad_lifted, lift_weight), mlp_gain.astype(jnp.float32), normed_two, scale_two
    )
    grad_mixed = grad_out + grad_mlp_norm
    mixed_low = grad_mixed.astype(jnp.bfloat16)
    proj_term = outer_sum(attended_low, mixed_low)
    grad_attended = back_dot(mixed_low, proj_weight).astype(jnp.bfloat16)
    grad_queries, grad_wide = attend_backward(
        queries, with_halo, log_totals, grad_attended, offset, lengths
    )
    rim_rows = jnp.concatenate([grad_wide[:HALF], grad_wide[row_count + HALF :]], axis=0)
    from_peers = with_halo_2(rim_rows.astype(jnp.bfloat16), (("ctx", 0),), HALF).astype(
        rim_rows.dtype
    )
    own_rows = grad_wide[HALF : row_count + HALF]
    own_rows = own_rows.at[:HALF].add(from_peers[:HALF])
    own_rows = own_rows.at[row_count - HALF :].add(from_peers[3 * HALF :])
    cosine_table, sine_table = rope_tables(offset + jnp.arange(row_count, dtype=jnp.int32))
    grad_query_flat = rotate(grad_queries, cosine_table, sine_table, -1.0).reshape(row_count, D)
    grad_keys = rotate(
        own_rows[:, 0].reshape(row_count, head_count, HD), cosine_table, sine_table, -1.0
    ).reshape(row_count, D)
    grad_packed = jnp.concatenate([grad_query_flat, grad_keys, own_rows[:, 1]], axis=1).astype(
        jnp.bfloat16
    )
    qkv_term = outer_sum(attn_input, grad_packed)
    grad_attn_norm, attn_gain_term = norm_back(
        back_dot(grad_packed, qkv_weight), attn_gain.astype(jnp.float32), normed_one, scale_one
    )
    grad_hidden = grad_mixed + grad_attn_norm
    return (
        grad_hidden.astype(jnp.bfloat16),
        (attn_gain_term, qkv_term, proj_term, mlp_gain_term, lift_term, down_term),
    )


def body(
    inputs,
    out_grad,
    doc_lengths,
    attn_gain,
    qkv_weight,
    proj_weight,
    mlp_gain,
    lift_weight,
    down_weight,
):
    on_first = lax.axis_index("section") == 0
    weights = (
        lax.all_gather(attn_gain[0], "fsdp", axis=0, tiled=True),
        lax.all_gather(qkv_weight[0], "fsdp", axis=0, tiled=True),
        lax.all_gather(proj_weight[0], "fsdp", axis=0, tiled=True),
        lax.all_gather(mlp_gain[0], "fsdp", axis=0, tiled=True),
        lax.all_gather(lift_weight[0], "fsdp", axis=0, tiled=True),
        lax.all_gather(down_weight[0], "fsdp", axis=0, tiled=True),
    )
    micro_count = inputs.shape[0]
    row_count = inputs.shape[2]
    offset = lax.axis_index("ctx") * row_count
    inbox = jnp.zeros((row_count, D), jnp.bfloat16)
    outputs = []
    saved_all = []
    length_rows = []
    for tick_index in range(micro_count + 1):
        lengths = jnp.where(
            on_first,
            doc_lengths[min(tick_index, micro_count - 1), 0],
            doc_lengths[max(tick_index - 1, 0), 0],
        )
        source = jnp.where(on_first, inputs[min(tick_index, micro_count - 1), 0], inbox)
        result, saved_state = forward_layer(source.astype(jnp.float32), weights, lengths, offset)
        outputs.append(result)
        saved_all.append(saved_state)
        length_rows.append(lengths)
        if tick_index < micro_count:
            inbox = shifted(result, "section", 1)
    acts = jnp.stack(
        [jnp.where(on_first, outputs[number], outputs[number + 1]) for number in range(micro_count)]
    )
    grad_inbox = jnp.zeros((row_count, D), jnp.bfloat16)
    totals = None
    grads_at = []
    for tick_index in range(micro_count + 1):
        position = micro_count - tick_index
        cotangent = (
            out_grad[micro_count - 1 - tick_index, 0]
            if tick_index < micro_count
            else jnp.zeros_like(grad_inbox)
        )
        incoming = jnp.where(on_first, grad_inbox, cotangent)
        grad_hidden, terms = backward_layer(
            incoming.astype(jnp.float32),
            saved_all[position],
            weights,
            length_rows[position],
            offset,
        )
        totals = (
            terms
            if totals is None
            else tuple((total_term + new_term for total_term, new_term in zip(totals, terms)))
        )
        grads_at.append(grad_hidden)
        if tick_index < micro_count:
            grad_inbox = shifted(grad_hidden, "section", -1)
    in_grads = jnp.stack(
        [
            jnp.where(on_first, grads_at[micro_count - number], grads_at[micro_count - 1 - number])
            for number in range(micro_count)
        ]
    )
    attn_total, qkv_total, proj_total, mlp_total, lift_total, down_total = totals
    shard_sums = (
        lax.psum_scatter(
            attn_total.astype(jnp.bfloat16), "fsdp", scatter_dimension=0, tiled=True
        ).astype(jnp.float32),
        lax.psum_scatter(
            qkv_total.astype(jnp.bfloat16), "fsdp", scatter_dimension=0, tiled=True
        ).astype(jnp.float32),
        lax.psum_scatter(
            proj_total.astype(jnp.bfloat16), "fsdp", scatter_dimension=0, tiled=True
        ).astype(jnp.float32),
        lax.psum_scatter(
            mlp_total.astype(jnp.bfloat16), "fsdp", scatter_dimension=0, tiled=True
        ).astype(jnp.float32),
        lax.psum_scatter(
            lift_total.astype(jnp.bfloat16), "fsdp", scatter_dimension=0, tiled=True
        ).astype(jnp.float32),
        lax.psum_scatter(
            down_total.astype(jnp.bfloat16), "fsdp", scatter_dimension=0, tiled=True
        ).astype(jnp.float32),
    )
    finals = (
        lax.psum(shard_sums[0].astype(jnp.bfloat16), "ctx").astype(jnp.float32),
        lax.psum(shard_sums[1].astype(jnp.bfloat16), "ctx").astype(jnp.float32),
        lax.psum(shard_sums[2].astype(jnp.bfloat16), "ctx").astype(jnp.float32),
        lax.psum(shard_sums[3].astype(jnp.bfloat16), "ctx").astype(jnp.float32),
        lax.psum(shard_sums[4].astype(jnp.bfloat16), "ctx").astype(jnp.float32),
        lax.psum(shard_sums[5].astype(jnp.bfloat16), "ctx").astype(jnp.float32),
    )
    return (
        acts[None, :, None],
        in_grads[None, :, None],
        finals[0][None],
        finals[1][None],
        finals[2][None],
        finals[3][None],
        finals[4][None],
        finals[5][None],
    )


def solution(mesh):
    placed = (
        P(None, "fsdp", "ctx", None),
        P(None, "fsdp", "ctx", None),
        P(None, "fsdp", None),
        P("section", "fsdp"),
        P("section", "fsdp", None),
        P("section", "fsdp", None),
        P("section", "fsdp"),
        P("section", "fsdp", None),
        P("section", "fsdp", None),
    )
    return jax.shard_map(
        body,
        mesh=mesh,
        in_specs=placed,
        out_specs=(
            P("section", None, "fsdp", "ctx", None),
            P("section", None, "fsdp", "ctx", None),
            P("section", "fsdp"),
            P("section", "fsdp", None),
            P("section", "fsdp", None),
            P("section", "fsdp"),
            P("section", "fsdp", None),
            P("section", "fsdp", None),
        ),
        check_vma=False,
    )
```

profile of v0, /device:TPU:1, one launch (start us, length us, event | category | flops | bytes accessed | tf_op | source)
XLA Modules:
  0.0 651.8 jit_solution(7718713026477477358)
XLA Ops:
  13.0 9.5 %all-reduce.7 = (bf16[768]{0:T(1024)(128)(2,1)S(1)}, bf16[768]{0:T(1024)(128)(2,1)S(1)}) all-reduce(bf16[768]{0:T(1024)(128)(2,1)S(1)} %dynamic-update-slice.18, bf16[768]{0:T(1024)(128)(2,1)S(1)} %dynamic-update-slice.19), channel_id=2, replica_groups=mesh['section'=2,'ctx'=16,'fsdp'=4] {'fsdp'}, use_global_device_ids=true, to_apply=%add | all-reduce | flops 1536 | bytes 6144
  24.4 31.5 %all-gather.11.cloned.1.call-done = bf16[1,768,2304]{2,1,0:T(8,128)(2,1)} async-done(((bf16[1,192,2304]{2,1,0:T(8,128)(2,1)}), bf16[1,768,2304]{2,1,0:T(8,128)(2,1)}) %all-gather.11.cloned.1.call-update) | async-done | bytes 3538960 | tf_op jit(solution)/shard_map/all_gather | solution.py:317
  55.8 2.7 fusion.22
  61.0 3.7 collective-permute-start
  64.8 1.9 collective-permute-start.1
  67.4 4.8 collective-permute-done.1
  75.2 6.0 all-gather.13.cloned.1.call-done
  83.1 44.1 %all-gather.15.cloned.1.call-done = bf16[1,768,2304]{2,1,0:T(8,128)(2,1)} async-done(((bf16[1,192,2304]{2,1,0:T(8,128)(2,1)}), bf16[1,768,2304]{2,1,0:T(8,128)(2,1)}) %all-gather.15.cloned.1.call-update) | async-done | bytes 3538960 | tf_op jit(solution)/shard_map/all_gather | solution.py:320
  127.2 2.7 fusion.10
  131.0 2.1 multiply_convert_fusion.8
  133.1 24.1 %all-gather.17.cloned.1.call-done = bf16[1,1152,768]{2,1,0:T(8,128)(2,1)} async-done(((bf16[1,288,768]{2,1,0:T(8,128)(2,1)}), bf16[1,1152,768]{2,1,0:T(8,128)(2,1)}) %all-gather.17.cloned.1.call-update) | async-done | bytes 1769488 | tf_op jit(solution)/shard_map/all_gather | solution.py:321
  159.1 4.6 collective-permute-start.2
  163.7 3.5 collective-permute-done.2
  167.6 2.7 fusion.20
  174.3 2.1 fusion.282
  177.6 4.6 collective-permute-start.3
  182.2 2.1 collective-permute-start.4
  184.8 4.4 collective-permute-done.4
  195.0 2.1 multiply_convert_fusion.7
  197.6 5.6 collective-permute-start.5
  203.3 2.6 collective-permute-done.5
  208.8 2.0 copy.133
  213.4 1.9 copy.134
  215.3 2.1 fusion.281
  219.8 3.9 collective-permute-start.6
  223.7 2.3 collective-permute-start.7
  226.8 3.9 collective-permute-done.7
  232.9 2.1 copy.135
  241.3 2.6 multiply_convert_fusion.5
  249.8 2.0 fusion.92
  256.6 1.9 collective-permute-start.8
  258.5 2.6 collective-permute-start.9
  263.2 4.7 collective-permute-done.9
  270.7 5.2 scatter-add.20
  275.9 2.7 slice_add_fusion.2
  278.7 6.1 scatter-add.21
  289.2 1.9 fusion.176
  294.9 4.9 collective-permute-done.10
  308.0 2.1 fusion.90
  314.8 4.1 collective-permute-start.11
  318.9 1.9 collective-permute-start.12
  321.6 2.0 collective-permute-done.11
  323.6 4.4 collective-permute-done.12
  330.8 5.2 scatter-add.24
  336.0 2.7 slice_add_fusion.1
  338.7 6.1 scatter-add.25
  349.3 2.0 fusion.184
  354.4 5.9 collective-permute-done.13
  373.8 2.3 fusion.219
  377.5 3.0 add_convert_fusion
  381.7 5.1 fusion.221
  386.8 4.1 fusion.220
  394.7 4.0 collective-permute-start.14
  398.7 1.9 collective-permute-start.15
  403.4 4.8 collective-permute-done.15
  408.9 6.3 scatter-add.26
  416.5 7.9 %scatter-add.29 = f32[128,2,768]{0,2,1:T(8,128)S(1)} dynamic-update-slice(f32[128,2,768]{0,2,1:T(8,128)S(1)} %scatter-add.26, f32[64,2,768]{0,2,1:T(8,128)} %slice_add_fusion, s32[]{:T(128)} %constant.385.clone.1, s32[]{:T(128)} %constant.373.clone.1, s32[]{:T(128)} %constant.373.clone.1) | dynamic-update-slice | bytes 786436 | tf_op jit(solution)/shard_map/scatter-add | solution.py:283
  426.0 8.1 %add_convert_fusion.1 = bf16[768,2304]{1,0:T(8,128)(2,1)} fusion(f32[768,2304]{1,0:T(8,128)} %fusion.221, f32[768,2304]{1,0:T(8,128)} %fusion.220, bf16[128,768]{0,1:T(8,128)(2,1)S(1)} %fusion.233, bf16[128,768]{0,1:T(8,128)(2,1)S(1)} %fusion.195, bf16[128,768]{0,1:T(8,128)(2,1)S(1)} %bitcast.387, f32[768]{0:T(1024)S(1)} %convert_element_type.376, ...), kind=kOutput, calls=%fused_computation.1 | convolution fusion | flops 460652544 | bytes 18486272 | tf_op jit(solution)/shard_map/dot_general | solution.py:85
  434.3 32.7 %reduce-scatter.9.cloned.1.call-done = bf16[192,2304]{1,0:T(8,128)(2,1)} async-done(((bf16[768,2304]{1,0:T(8,128)(2,1)}), bf16[192,2304]{1,0:T(8,128)(2,1)}) %reduce-scatter.9.cloned.1.call-update) | async-done | bytes 884752 | tf_op jit(solution)/shard_map/reduce_scatter | solution.py:392
  467.0 43.8 %reduce-scatter.5.cloned.1.call-done = bf16[192,2304]{1,0:T(8,128)(2,1)} async-done(((bf16[768,2304]{1,0:T(8,128)(2,1)}), bf16[192,2304]{1,0:T(8,128)(2,1)}) %reduce-scatter.5.cloned.1.call-update) | async-done | bytes 884752 | tf_op jit(solution)/shard_map/reduce_scatter | solution.py:383
  515.5 6.7 %all-reduce.6 = (bf16[768]{0:T(1024)(128)(2,1)S(1)}, bf16[768]{0:T(1024)(128)(2,1)S(1)}) all-reduce(bf16[768]{0:T(1024)(128)(2,1)S(1)} %add_convert_fusion.7, bf16[768]{0:T(1024)(128)(2,1)S(1)} %add_convert_fusion.6), channel_id=8, replica_groups=mesh['section'=2,'ctx'=16,'fsdp'=4] {'fsdp'}, use_global_device_ids=true, to_apply=%region_45.46.clone | all-reduce | flops 1536 | bytes 6144
  522.3 29.3 %all-reduce.4 = (bf16[1,192]{1,0:T(2,128)(2,1)S(1)}, bf16[1,192]{1,0:T(2,128)(2,1)S(1)}) all-reduce(bf16[1,192]{1,0:T(2,128)(2,1)S(1)} %broadcast_in_dim.308, bf16[1,192]{1,0:T(2,128)(2,1)S(1)} %broadcast_in_dim.314), channel_id=1, replica_groups=mesh['section'=2,'ctx'=16,'fsdp'=4] {'ctx'}, use_global_device_ids=true, to_apply=%region_46.47 | all-reduce | flops 384 | bytes 1536 | tf_op jit(solution)/shard_map/psum | solution.py:400
  553.7 84.3 %all-reduce.10.cloned.1.call-done = (bf16[1,192,2304]{2,1,0:T(8,128)(2,1)}, bf16[1,192,768]{2,1,0:T(8,128)(2,1)}, bf16[1,192,2304]{2,1,0:T(8,128)(2,1)}, bf16[1,288,768]{2,1,0:T(8,128)(2,1)}) async-done(((bf16[1,192,2304]{2,1,0:T(8,128)(2,1)}, bf16[1,192,768]{2,1,0:T(8,128)(2,1)}, bf16[1,192,2304]{2,1,0:T(8,128)(2,1)}, bf16[1,288,768]{2,1,0:T(8,128)(2,1)}), (bf16[1,192,2304]{2,1,0:T(8,128)(2,1)}, ...) | async-done | bytes 2506768 | tf_op jit(solution)/shard_map/psum | solution.py:401
  639.9 2.6 broadcast_in_dim.311
  (620 shorter events, 129.8 us)
Async XLA Ops:
  7.2 48.6 %all-gather.11.cloned.1.call-start = ((), (), s32[]{:S(2)}) async-start(), calls=%async_computation.8 | async-start | bytes 4423680 | tf_op jit(solution)/shard_map/all_gather | solution.py:317
  8.0 73.2 %all-gather.13.cloned.1.call-start = ((), (), s32[]{:S(2)}) async-start(), calls=%async_computation.9 | async-start | bytes 1474560 | tf_op jit(solution)/shard_map/all_gather | solution.py:318
  8.7 118.5 %all-gather.15.cloned.1.call-start = ((), (), s32[]{:S(2)}) async-start(), calls=%async_computation.10 | async-start | bytes 4423680 | tf_op jit(solution)/shard_map/all_gather | solution.py:320
  9.4 147.7 %all-gather.17.cloned.1.call-start = ((), (), s32[]{:S(2)}) async-start(), calls=%async_computation.11 | async-start | bytes 2211840 | tf_op jit(solution)/shard_map/all_gather | solution.py:321
  10.0 424.2 %reduce-scatter.7.cloned.1.call-start = ((), (), s32[]{:S(2)}) async-start(), calls=%async_computation.5 | async-start | bytes 1474560 | tf_op jit(solution)/shard_map/reduce_scatter | solution.py:386
  10.6 47.9 %copy-start.165 = (f32[128]{0:T(128)}, f32[128]{0:T(128)S(1)}, u32[]{:S(2)}) copy-start(f32[128]{0:T(128)S(1)} %broadcast_multiply_fusion.22) | copy-start | bytes 1540
  10.8 47.7 %copy-start.179 = (f32[128]{0:T(128)}, f32[128]{0:T(128)S(1)}, u32[]{:S(2)}) copy-start(f32[128]{0:T(128)S(1)} %add_rsqrt_fusion.5) | copy-start | bytes 1540
  23.3 161.0 %copy-start.59 = (f32[128,64]{0,1:T(8,128)}, f32[128,64]{0,1:T(8,128)S(1)}, u32[]{:S(2)}) copy-start(f32[128,64]{0,1:T(8,128)S(1)} %get-tuple-element.368) | copy-start | bytes 98308
  23.3 161.0 %copy-start.71 = (f32[128,64]{0,1:T(8,128)}, f32[128,64]{0,1:T(8,128)S(1)}, u32[]{:S(2)}) copy-start(f32[128,64]{0,1:T(8,128)S(1)} %get-tuple-element.369) | copy-start | bytes 98308
  23.5 150.7 %copy-start.45 = (f32[128,768]{1,0:T(8,128)}, f32[128,768]{1,0:T(8,128)S(1)}, u32[]{:S(2)}) copy-start(f32[128,768]{1,0:T(8,128)S(1)} %copy.120) | copy-start | bytes 1179652
  61.0 6.3 collective-permute-start
  64.8 7.4 %collective-permute-start.1 = (bf16[64,2,768]{2,0,1:T(8,128)(2,1)S(1)}, bf16[64,2,768]{2,0,1:T(8,128)(2,1)S(1)}, u32[]{:S(2)}, u32[]{:S(2)}) collective-permute-start(bf16[64,2,768]{2,0,1:T(8,128)(2,1)S(1)} %get-tuple-element.358), channel_id=1, source_target_pairs={{4,0},{8,4},{12,8},{16,12},{20,16},{24,20},{28,24},{32,28},{36,32}... | collective-permute-start | bytes 589832 | tf_op jit(solution)/shard_map/ppermute | solution.py:29
  75.2 54.7 %copy-start.105 = (bf16[12,64,128]{2,1,0:T(8,128)(2,1)}, bf16[12,64,128]{2,1,0:T(8,128)(2,1)S(1)}, u32[]{:S(2)}) copy-start(bf16[12,64,128]{2,1,0:T(8,128)(2,1)S(1)} %convolution_convert_fusion.2) | copy-start | bytes 589828
  82.9 74.3 %copy-start.20 = (f32[128,768]{1,0:T(8,128)}, f32[128,768]{1,0:T(8,128)S(1)}, u32[]{:S(2)}) copy-start(f32[128,768]{1,0:T(8,128)S(1)} %get-tuple-element.380) | copy-start | bytes 1179652
  82.9 47.0 %copy-start.167 = (f32[128]{0:T(128)}, f32[128]{0:T(128)S(1)}, u32[]{:S(2)}) copy-start(f32[128]{0:T(128)S(1)} %broadcast_multiply_fusion.21) | copy-start | bytes 1540
  83.1 46.8 %copy-start.181 = (f32[128]{0:T(128)}, f32[128]{0:T(128)S(1)}, u32[]{:S(2)}) copy-start(f32[128]{0:T(128)S(1)} %add_rsqrt_fusion.4) | copy-start | bytes 1540
  133.1 34.3 %copy-start.66 = (bf16[128,1152]{1,0:T(8,128)(2,1)}, bf16[128,1152]{1,0:T(8,128)(2,1)S(1)}, u32[]{:S(2)}) copy-start(bf16[128,1152]{1,0:T(8,128)(2,1)S(1)} %get-tuple-element.306) | copy-start | bytes 884740
  159.1 8.2 %collective-permute-start.2 = (bf16[128,768]{1,0:T(8,128)(2,1)S(1)}, bf16[128,768]{1,0:T(8,128)(2,1)S(1)}, u32[]{:S(2)}, u32[]{:S(2)}) collective-permute-start(bf16[128,768]{1,0:T(8,128)(2,1)S(1)} %fusion.79), channel_id=1, source_target_pairs={{0,64},{1,65},{2,66},{3,67},{4,68},{5,69},{6,70},{7,71},{8,72},{9,... | collective-permute-start | bytes 589832 | tf_op jit(solution)/shard_map/ppermute | solution.py:37
  167.4 24.8 %copy-start.30 = (bf16[128,768]{1,0:T(8,128)(2,1)}, bf16[128,768]{1,0:T(8,128)(2,1)S(1)}, u32[]{:S(2)}) copy-start(bf16[128,768]{1,0:T(8,128)(2,1)S(1)} %get-tuple-element.305) | copy-start | bytes 589828
  177.6 7.2 %collective-permute-start.3 = (bf16[64,2,768]{2,0,1:T(8,128)(2,1)S(1)}, bf16[64,2,768]{2,0,1:T(8,128)(2,1)S(1)}, u32[]{:S(2)}, u32[]{:S(2)}) collective-permute-start(bf16[64,2,768]{2,0,1:T(8,128)(2,1)S(1)} %get-tuple-element.351), channel_id=1, source_target_pairs={{0,4},{4,8},{8,12},{12,16},{16,20},{20,24},{24,28},{28,32},{32,36}... | collective-permute-start | bytes 589832 | tf_op jit(solution)/shard_map/ppermute | solution.py:26
  182.2 7.0 %collective-permute-start.4 = (bf16[64,2,768]{2,0,1:T(8,128)(2,1)S(1)}, bf16[64,2,768]{2,0,1:T(8,128)(2,1)S(1)}, u32[]{:S(2)}, u32[]{:S(2)}) collective-permute-start(bf16[64,2,768]{2,0,1:T(8,128)(2,1)S(1)} %get-tuple-element.352), channel_id=1, source_target_pairs={{4,0},{8,4},{12,8},{16,12},{20,16},{24,20},{28,24},{32,28},{36,32}... | collective-permute-start | bytes 589832 | tf_op jit(solution)/shard_map/ppermute | solution.py:29
  195.0 11.2 %copy-start.5 = (bf16[1,768,2304]{2,1,0:T(8,128)(2,1)S(1)}, bf16[1,768,2304]{2,1,0:T(8,128)(2,1)}, u32[]{:S(2)}) copy-start(bf16[1,768,2304]{2,1,0:T(8,128)(2,1)} %all-gather.11.cloned.1.call-done) | copy-start | bytes 10616836
  197.2 8.7 %copy-start.34 = (bf16[2,1,128,768]{3,2,1,0:T(8,128)(2,1)S(1)}, bf16[2,1,128,768]{3,2,1,0:T(8,128)(2,1)}, u32[]{:S(2)}) copy-start(bf16[2,1,128,768]{3,2,1,0:T(8,128)(2,1)} %param.21) | copy-start | bytes 1179652
  197.6 8.6 %copy-start.85 = (bf16[128,768]{1,0:T(8,128)(2,1)}, bf16[128,768]{1,0:T(8,128)(2,1)S(1)}, u32[]{:S(2)}) copy-start(bf16[128,768]{1,0:T(8,128)(2,1)S(1)} %fusion.76) | copy-start | bytes 589828
  197.6 8.2 %collective-permute-start.5 = (bf16[128,768]{1,0:T(8,128)(2,1)S(1)}, bf16[128,768]{1,0:T(8,128)(2,1)S(1)}, u32[]{:S(2)}, u32[]{:S(2)}) collective-permute-start(bf16[128,768]{1,0:T(8,128)(2,1)S(1)} %fusion.76), channel_id=1, source_target_pairs={{0,64},{1,65},{2,66},{3,67},{4,68},{5,69},{6,70},{7,71},{8,72},{9,... | collective-permute-start | bytes 589832 | tf_op jit(solution)/shard_map/ppermute | solution.py:37
  218.6 12.1 %copy-start.83 = (bf16[128,1,768]{2,0,1:T(8,128)(2,1)S(1)}, bf16[128,1,768]{2,0,1:T(8,128)(2,1)}, u32[]{:S(2)}) copy-start(bf16[128,1,768]{2,0,1:T(8,128)(2,1)} %fusion.230) | copy-start | bytes 589828
  218.6 12.1 %copy-start.84 = (bf16[128,1,768]{2,0,1:T(8,128)(2,1)S(1)}, bf16[128,1,768]{2,0,1:T(8,128)(2,1)}, u32[]{:S(2)}) copy-start(bf16[128,1,768]{2,0,1:T(8,128)(2,1)} %get-tuple-element.310) | copy-start | bytes 589828
  219.8 7.0 %collective-permute-start.6 = (bf16[64,2,768]{2,0,1:T(8,128)(2,1)S(1)}, bf16[64,2,768]{2,0,1:T(8,128)(2,1)S(1)}, u32[]{:S(2)}, u32[]{:S(2)}) collective-permute-start(bf16[64,2,768]{2,0,1:T(8,128)(2,1)S(1)} %get-tuple-element.345), channel_id=1, source_target_pairs={{0,4},{4,8},{8,12},{12,16},{16,20},{20,24},{24,28},{28,32},{32,36}... | collective-permute-start | bytes 589832 | tf_op jit(solution)/shard_map/ppermute | solution.py:26
  223.7 7.0 %collective-permute-start.7 = (bf16[64,2,768]{2,0,1:T(8,128)(2,1)S(1)}, bf16[64,2,768]{2,0,1:T(8,128)(2,1)S(1)}, u32[]{:S(2)}, u32[]{:S(2)}) collective-permute-start(bf16[64,2,768]{2,0,1:T(8,128)(2,1)S(1)} %get-tuple-element.346), channel_id=1, source_target_pairs={{4,0},{8,4},{12,8},{16,12},{20,16},{24,20},{28,24},{32,28},{36,32}... | collective-permute-start | bytes 589832 | tf_op jit(solution)/shard_map/ppermute | solution.py:29
  238.9 134.3 %copy-start.18 = (f32[128,768]{1,0:T(8,128)}, f32[128,768]{1,0:T(8,128)S(1)}, u32[]{:S(2)}) copy-start(f32[128,768]{1,0:T(8,128)S(1)} %get-tuple-element.388) | copy-start | bytes 1179652
  256.6 6.6 %collective-permute-start.8 = (bf16[64,2,768]{0,2,1:T(8,128)(2,1)S(1)}, bf16[64,2,768]{0,2,1:T(8,128)(2,1)S(1)}, u32[]{:S(2)}, u32[]{:S(2)}) collective-permute-start(bf16[64,2,768]{0,2,1:T(8,128)(2,1)S(1)} %get-tuple-element.319), channel_id=1, source_target_pairs={{0,4},{4,8},{8,12},{12,16},{16,20},{20,24},{24,28},{28,32},{32,36}... | collective-permute-start | bytes 589832 | tf_op jit(solution)/shard_map/ppermute | solution.py:26
  258.5 9.4 %collective-permute-start.9 = (bf16[64,2,768]{0,2,1:T(8,128)(2,1)S(1)}, bf16[64,2,768]{0,2,1:T(8,128)(2,1)S(1)}, u32[]{:S(2)}, u32[]{:S(2)}) collective-permute-start(bf16[64,2,768]{0,2,1:T(8,128)(2,1)S(1)} %get-tuple-element.320), channel_id=1, source_target_pairs={{4,0},{8,4},{12,8},{16,12},{20,16},{24,20},{28,24},{32,28},{36,32}... | collective-permute-start | bytes 589832 | tf_op jit(solution)/shard_map/ppermute | solution.py:29
  291.2 8.6 %copy-start.96 = (bf16[2,1,128,768]{3,2,1,0:T(8,128)(2,1)S(1)}, bf16[2,1,128,768]{3,2,1,0:T(8,128)(2,1)}, u32[]{:S(2)}) copy-start(bf16[2,1,128,768]{3,2,1,0:T(8,128)(2,1)} %param.22) | copy-start | bytes 1179652
  291.4 8.4 %copy-start.119 = (bf16[128,768]{1,0:T(8,128)(2,1)}, bf16[128,768]{1,0:T(8,128)(2,1)S(1)}, u32[]{:S(2)}) copy-start(bf16[128,768]{1,0:T(8,128)(2,1)S(1)} %fusion.175) | copy-start | bytes 589828
  291.4 8.4 %copy-start.15 = (bf16[1,1152,768]{2,1,0:T(8,128)(2,1)S(1)}, bf16[1,1152,768]{2,1,0:T(8,128)(2,1)}, u32[]{:S(2)}) copy-start(bf16[1,1152,768]{2,1,0:T(8,128)(2,1)} %all-gather.17.cloned.1.call-done) | copy-start | bytes 5308420
  291.4 8.4 %copy-start.52 = (f32[128,2304]{1,0:T(8,128)S(1)}, f32[128,2304]{1,0:T(8,128)}, u32[]{:S(2)}) copy-start(f32[128,2304]{1,0:T(8,128)} %copy-done.51) | copy-start | bytes 3538948
  291.4 8.4 %copy-start.136 = (f32[128,1152]{1,0:T(8,128)S(1)}, f32[128,1152]{1,0:T(8,128)}, u32[]{:S(2)}) copy-start(f32[128,1152]{1,0:T(8,128)} %get-tuple-element.303) | copy-start | bytes 1769476
  291.4 8.3 %collective-permute-start.10 = (bf16[128,768]{1,0:T(8,128)(2,1)S(1)}, bf16[128,768]{1,0:T(8,128)(2,1)S(1)}, u32[]{:S(2)}, u32[]{:S(2)}) collective-permute-start(bf16[128,768]{1,0:T(8,128)(2,1)S(1)} %fusion.175), channel_id=1, source_target_pairs={{64,0},{65,1},{66,2},{67,3},{68,4},{69,5},{70,6},{71,7},{72,8},{73... | collective-permute-start | bytes 589832 | tf_op jit(solution)/shard_map/ppermute | solution.py:37
  314.8 8.8 %collective-permute-start.11 = (bf16[64,2,768]{0,2,1:T(8,128)(2,1)S(1)}, bf16[64,2,768]{0,2,1:T(8,128)(2,1)S(1)}, u32[]{:S(2)}, u32[]{:S(2)}) collective-permute-start(bf16[64,2,768]{0,2,1:T(8,128)(2,1)S(1)} %get-tuple-element.317), channel_id=1, source_target_pairs={{0,4},{4,8},{8,12},{12,16},{16,20},{20,24},{24,28},{28,32},{32,36}... | collective-permute-start | bytes 589832 | tf_op jit(solution)/shard_map/ppermute | solution.py:26
  318.9 9.1 %collective-permute-start.12 = (bf16[64,2,768]{0,2,1:T(8,128)(2,1)S(1)}, bf16[64,2,768]{0,2,1:T(8,128)(2,1)S(1)}, u32[]{:S(2)}, u32[]{:S(2)}) collective-permute-start(bf16[64,2,768]{0,2,1:T(8,128)(2,1)S(1)} %get-tuple-element.318), channel_id=1, source_target_pairs={{4,0},{8,4},{12,8},{16,12},{20,16},{24,20},{28,24},{32,28},{36,32}... | collective-permute-start | bytes 589832 | tf_op jit(solution)/shard_map/ppermute | solution.py:29
  351.3 9.1 %copy-start.135 = (f32[128,1152]{1,0:T(8,128)S(1)}, f32[128,1152]{1,0:T(8,128)}, u32[]{:S(2)}) copy-start(f32[128,1152]{1,0:T(8,128)} %get-tuple-element.307) | copy-start | bytes 1769476
  352.2 9.0 %copy-start.117 = (bf16[128,768]{1,0:T(8,128)(2,1)}, bf16[128,768]{1,0:T(8,128)(2,1)S(1)}, u32[]{:S(2)}) copy-start(bf16[128,768]{1,0:T(8,128)(2,1)S(1)} %get-tuple-element.297) | copy-start | bytes 589828
  352.2 8.2 %copy-start.16 = (bf16[1,1152,768]{2,1,0:T(8,128)(2,1)S(1)}, bf16[1,1152,768]{2,1,0:T(8,128)(2,1)}, u32[]{:S(2)}) copy-start(bf16[1,1152,768]{2,1,0:T(8,128)(2,1)} %all-gather.17.cloned.1.call-done) | copy-start | bytes 5308420
  352.2 8.2 %copy-start.50 = (f32[128,2304]{1,0:T(8,128)S(1)}, f32[128,2304]{1,0:T(8,128)}, u32[]{:S(2)}) copy-start(f32[128,2304]{1,0:T(8,128)} %copy-done.49) | copy-start | bytes 3538948
  352.2 8.2 %collective-permute-start.13 = (bf16[128,768]{1,0:T(8,128)(2,1)S(1)}, bf16[128,768]{1,0:T(8,128)(2,1)S(1)}, u32[]{:S(2)}, u32[]{:S(2)}) collective-permute-start(bf16[128,768]{1,0:T(8,128)(2,1)S(1)} %get-tuple-element.297), channel_id=1, source_target_pairs={{64,0},{65,1},{66,2},{67,3},{68,4},{69,5},{70,6},{71,7},{72,8},{73... | collective-permute-start | bytes 589832 | tf_op jit(solution)/shard_map/ppermute | solution.py:37
  367.1 67.1 %reduce-scatter.11.cloned.1.call-start = ((), (), s32[]{:S(2)}) async-start(), calls=%async_computation.7 | async-start | bytes 2211840 | tf_op jit(solution)/shard_map/reduce_scatter | solution.py:395
  373.2 93.8 %reduce-scatter.9.cloned.1.call-start = ((), (), s32[]{:S(2)}) async-start(), calls=%async_computation.6 | async-start | bytes 4423680 | tf_op jit(solution)/shard_map/reduce_scatter | solution.py:392
  380.6 130.2 %reduce-scatter.5.cloned.1.call-start = ((), (), s32[]{:S(2)}) async-start(), calls=%async_computation.4 | async-start | bytes 4423680 | tf_op jit(solution)/shard_map/reduce_scatter | solution.py:383
  394.7 8.7 %collective-permute-start.14 = (bf16[64,2,768]{0,2,1:T(8,128)(2,1)S(1)}, bf16[64,2,768]{0,2,1:T(8,128)(2,1)S(1)}, u32[]{:S(2)}, u32[]{:S(2)}) collective-permute-start(bf16[64,2,768]{0,2,1:T(8,128)(2,1)S(1)} %get-tuple-element.315), channel_id=1, source_target_pairs={{0,4},{4,8},{8,12},{12,16},{16,20},{20,24},{24,28},{28,32},{32,36}... | collective-permute-start | bytes 589832 | tf_op jit(solution)/shard_map/ppermute | solution.py:26
  398.7 9.5 %collective-permute-start.15 = (bf16[64,2,768]{0,2,1:T(8,128)(2,1)S(1)}, bf16[64,2,768]{0,2,1:T(8,128)(2,1)S(1)}, u32[]{:S(2)}, u32[]{:S(2)}) collective-permute-start(bf16[64,2,768]{0,2,1:T(8,128)(2,1)S(1)} %get-tuple-element.316), channel_id=1, source_target_pairs={{4,0},{8,4},{12,8},{16,12},{20,16},{24,20},{28,24},{32,28},{36,32}... | collective-permute-start | bytes 589832 | tf_op jit(solution)/shard_map/ppermute | solution.py:29
  416.5 8.0 %copy-start.63 = (f32[128,64]{0,1:T(8,128)S(1)}, f32[128,64]{0,1:T(8,128)}, u32[]{:S(2)}) copy-start(f32[128,64]{0,1:T(8,128)} %copy-done.59) | copy-start | bytes 98308
  416.5 8.0 %copy-start.113 = (f32[128,12,32]{0,2,1:T(8,128)S(1)}, f32[128,12,32]{0,2,1:T(8,128)}, u32[]{:S(2)}) copy-start(f32[128,12,32]{0,2,1:T(8,128)} %get-tuple-element.331) | copy-start | bytes 589828
  416.5 8.0 %copy-start.114 = (f32[128,12,32]{0,2,1:T(8,128)S(1)}, f32[128,12,32]{0,2,1:T(8,128)}, u32[]{:S(2)}) copy-start(f32[128,12,32]{0,2,1:T(8,128)} %get-tuple-element.332) | copy-start | bytes 589828
  416.5 8.0 %copy-start.139 = (f32[128,64]{0,1:T(8,128)S(1)}, f32[128,64]{0,1:T(8,128)}, u32[]{:S(2)}) copy-start(f32[128,64]{0,1:T(8,128)} %get-tuple-element.367) | copy-start | bytes 98308
  424.7 9.4 %copy-start.99 = (bf16[128,12,64]{0,2,1:T(8,128)(2,1)}, bf16[128,12,64]{0,2,1:T(8,128)(2,1)S(1)}, u32[]{:S(2)}) copy-start(bf16[128,12,64]{0,2,1:T(8,128)(2,1)S(1)} %get-tuple-element.361) | copy-start | bytes 589828
  434.1 77.3 %copy-start.86 = (bf16[128,768]{1,0:T(8,128)(2,1)S(1)}, bf16[128,768]{1,0:T(8,128)(2,1)}, u32[]{:S(2)}) copy-start(bf16[128,768]{1,0:T(8,128)(2,1)} %copy-done.85) | copy-start | bytes 589828
  434.1 77.3 %copy-start.131 = (bf16[128,768]{1,0:T(8,128)(2,1)S(1)}, bf16[128,768]{1,0:T(8,128)(2,1)}, u32[]{:S(2)}) copy-start(bf16[128,768]{1,0:T(8,128)(2,1)} %copy-done.130) | copy-start | bytes 589828
  434.1 77.4 %copy-start.17 = (bf16[1,1152,768]{2,1,0:T(8,128)(2,1)S(1)}, bf16[1,1152,768]{2,1,0:T(8,128)(2,1)}, u32[]{:S(2)}) copy-start(bf16[1,1152,768]{2,1,0:T(8,128)(2,1)} %all-gather.17.cloned.1.call-done) | copy-start | bytes 5308420
  434.1 77.4 %copy-start.19 = (f32[128,768]{1,0:T(8,128)S(1)}, f32[128,768]{1,0:T(8,128)}, u32[]{:S(2)}) copy-start(f32[128,768]{1,0:T(8,128)} %copy-done.18) | copy-start | bytes 1179652
  434.1 77.4 %copy-start.65 = (bf16[128,1152]{1,0:T(8,128)(2,1)S(1)}, bf16[128,1152]{1,0:T(8,128)(2,1)}, u32[]{:S(2)}) copy-start(bf16[128,1152]{1,0:T(8,128)(2,1)} %copy-done.64) | copy-start | bytes 884740
  434.2 203.9 %all-reduce.10.cloned.1.call-start = ((), (), s32[]{:S(2)}) async-start(), calls=%async_computation.12 | async-start | bytes 5013504 | tf_op jit(solution)/shard_map/psum | solution.py:401
  513.9 38.8 %copy-start.38 = (f32[128,768]{1,0:T(8,128)S(1)}, f32[128,768]{1,0:T(8,128)}, u32[]{:S(2)}) copy-start(f32[128,768]{1,0:T(8,128)} %copy-done.36) | copy-start | bytes 1179652
  513.9 38.8 %copy-start.118 = (bf16[128,768]{1,0:T(8,128)(2,1)S(1)}, bf16[128,768]{1,0:T(8,128)(2,1)}, u32[]{:S(2)}) copy-start(bf16[128,768]{1,0:T(8,128)(2,1)} %copy-done.117) | copy-start | bytes 589828
  515.4 37.5 %copy-start.121 = (bf16[1,128,768]{2,1,0:T(8,128)(2,1)S(1)}, bf16[1,128,768]{2,1,0:T(8,128)(2,1)}, u32[]{:S(2)}) copy-start(bf16[1,128,768]{2,1,0:T(8,128)(2,1)} %get-tuple-element.296) | copy-start | bytes 589828
  (154 other events, 363.2 us)
Sparse Core Ops, SparseCore 0:
  9.7 46.0 all-gather.10
  57.5 23.6 all-gather.12
  82.8 44.3 all-gather.14
  128.7 28.3 all-gather.16
  367.3 25.0 reduce-scatter.6
  395.2 27.9 reduce-scatter.10
  425.7 41.2 reduce-scatter.8
  469.5 41.1 reduce-scatter.4
  513.8 124.2 all-reduce.9
where the time goes:
time: 661 us; the launch traced here: 652 us
  waiting for transfers between devices  319 us (48%)
  local copies, waits for them, and re-layouts  86.9 us (13%)
  matrix products  79.3 us (12%)
  other arithmetic  53.8 us (8%)
  starting transfers between devices  49.1 us (7%)
  blocking collectives  45.5 us (7%)
  between operations  18.5 us (3%)
    psum x1, waiting for transfers between devices, body(): lax.psum(shard_sums[1].astype(jnp.bfloat16), 'ctx').astype(jnp.float32)  84.3 us
    all_gather x1, waiting for transfers between devices, body(): lax.all_gather(lift_weight[0], 'fsdp', axis=0, tiled=True)  44.1 us
    reduce_scatter x1, waiting for transfers between devices, body(): lax.psum_scatter(qkv_total.astype(jnp.bfloat16), 'fsdp', scatter_dimensio...  43.8 us
    reduce_scatter x1, waiting for transfers between devices, body(): lax.psum_scatter(lift_total.astype(jnp.bfloat16), 'fsdp', scatter_dimensi...  32.7 us
    all_gather x1, waiting for transfers between devices, body(): lax.all_gather(qkv_weight[0], 'fsdp', axis=0, tiled=True)  31.5 us
    dot_general x12, matrix products, outer_sum(): lax.dot_general(left, right, (((0,), (0,)), ((), ())), preferred_element_...  30.8 us
    psum x1, blocking collectives, body(): lax.psum(shard_sums[0].astype(jnp.bfloat16), 'ctx').astype(jnp.float32)  29.3 us
    ppermute x6, waiting for transfers between devices, with_halo_2(): lax.ppermute(lax.slice_in_dim(block, 0, width, axis=dim), axis, backward)  27 us
  transfers between devices with their start and end apart: 25, of which 22 were waited for; matrix products, arithmetic and copies ran while one was open for 12% of the time, Pallas kernels for 0%

commit v1 on v0

v1 whole, which is shorter than its diff:
```python
import functools

import jax
import jax.numpy as jnp
from jax import lax
from jax.experimental import pallas as pl
from jax.experimental.pallas import tpu as pltpu
from jax.sharding import PartitionSpec as P

D = 768
HD = 64
HALF = 64
SEQ_LEN = 2048
FF = 1152
WIDE = 2304
ROWS = 128
EXT = ROWS + 2 * HALF
MICRO = 2
OWN = MICRO * ROWS
SHARDS = 4
TILES = D // 128
norm_eps = 1e-05
rope_base = 10000.0
masked_score = -1e30
root_half = 0.7071067811865476
inv_root_tau = 0.3989422804014327
F32 = jnp.float32
BF16 = jnp.bfloat16


def mm(left, right):
    return lax.dot_general(left, right, (((1,), (0,)), ((), ())), preferred_element_type=F32)


def mm_nt(left, right):
    return lax.dot_general(left, right, (((1,), (1,)), ((), ())), preferred_element_type=F32)


def mm_tn(left, right):
    return lax.dot_general(left, right, (((0,), (0,)), ((), ())), preferred_element_type=F32)


def norm_parts(hidden):
    centre = hidden - jnp.mean(hidden, axis=-1, keepdims=True)
    inv_scale = lax.rsqrt(jnp.mean(centre * centre, axis=-1, keepdims=True) + norm_eps)
    return centre * inv_scale, inv_scale


def norm_back(grad_out, gain, normed, inv_scale):
    grad_normed = grad_out * gain
    inner = (
        grad_normed
        - jnp.mean(grad_normed, axis=-1, keepdims=True)
        - normed * jnp.mean(grad_normed * normed, axis=-1, keepdims=True)
    )
    return inner * inv_scale


def lane_is_low(shape, period):
    return lax.broadcasted_iota(jnp.int32, shape, 1) % period < period // 2


def turn(x):
    return jnp.where(lane_is_low(x.shape, HD), pltpu.roll(x, 96, 1), pltpu.roll(x, 32, 1))


def rotate(x, cosine, sine):
    return x * cosine + turn(x) * sine


def rotate_back(x, cosine, sine):
    return x * cosine - turn(x) * sine


def stack_heads(x):
    low = lane_is_low(x.shape, 128)
    zero = jnp.zeros_like(x)
    return jnp.concatenate([jnp.where(low, x, zero), jnp.where(low, zero, x)], axis=0)


def join_heads(x):
    half = x.shape[0] // 2
    low = lane_is_low((half, 128), 128)
    return jnp.where(low, x[:half], x[half:])


def start_weights(packed, buffers, sems, wanted):
    qkv, proj, lift, down = buffers
    waits = {}

    def go(name, index, src, dst):
        copy = pltpu.make_async_copy(src, dst, sems.at[index])
        copy.start()
        waits.setdefault(name, []).append(copy)

    shard_rows = packed.shape[0] // SHARDS
    for name in wanted:
        for f in range(SHARDS):
            at = f * shard_rows
            if name == "qkv":
                go(name, f, packed.at[pl.ds(at, 192)], qkv.at[pl.ds(f * 192, 192)])
            if name == "lift":
                go(name, 4 + f, packed.at[pl.ds(at + 192, 192)], lift.at[pl.ds(f * 192, 192)])
            for block in range(3):
                cols = pl.ds(block * D, D)
                if name == "proj":
                    go(
                        name,
                        8 + 3 * f + block,
                        packed.at[pl.ds(at + 384, 64), cols],
                        proj.at[pl.ds(f * 192 + block * 64, 64)],
                    )
                if name == "down":
                    go(
                        name,
                        20 + 3 * f + block,
                        packed.at[pl.ds(at + 448, 96), cols],
                        down.at[pl.ds(f * 288 + block * 96, 96)],
                    )
    return waits


def finish(waits, name):
    for copy in waits[name]:
        copy.wait()


def load_stream(flag, own, low, high, other, ext):
    for m in range(MICRO):
        for ref, alt, start, size in (
            (low, other[1], 0, HALF),
            (own, other[0], HALF, ROWS),
            (high, other[2], HALF + ROWS, HALF),
        ):
            value = ref[m]
            if alt is not None:
                value = jnp.where(flag, value, alt[m])
            ext[pl.ds(m * EXT + start, size), :] = value


def own_rows(x):
    return jnp.concatenate([x[HALF : HALF + ROWS], x[EXT + HALF : EXT + HALF + ROWS]], axis=0)


def forward_attention(ext, gain, wqkv, cos_ref, sin_ref, bias_ref, a_ext, q_ref, k_ref, v_ref, p_ref, o_ref):
    normed, _ = norm_parts(ext[...].astype(F32))
    a_ext[...] = (normed * gain).astype(BF16)
    a_own = own_rows(a_ext[...])
    cosine, sine = cos_ref[...], sin_ref[...]
    cos_own, sin_own = cosine[HALF : HALF + ROWS], sine[HALF : HALF + ROWS]
    for t in range(3):
        queries = mm(a_own, wqkv[:, 256 * t : 256 * t + 256])
        for s in range(2):
            cols = pl.ds(256 * t + 128 * s, 128)
            for m in range(MICRO):
                part = queries[m * ROWS : (m + 1) * ROWS, 128 * s : 128 * s + 128]
                q_ref[pl.ds(m * ROWS, ROWS), cols] = rotate(part, cos_own, sin_own).astype(
                    BF16
                ) * jnp.asarray(0.125, BF16)
        keys = mm(a_ext[...], wqkv[:, D + 256 * t : D + 256 * t + 256])
        for s in range(2):
            cols = pl.ds(256 * t + 128 * s, 128)
            for m in range(MICRO):
                part = keys[m * EXT : (m + 1) * EXT, 128 * s : 128 * s + 128]
                k_ref[pl.ds(m * EXT, EXT), cols] = rotate(part, cosine, sine).astype(BF16)
        values = mm(a_ext[...], wqkv[:, 2 * D + 256 * t : 2 * D + 256 * t + 256])
        v_ref[:, pl.ds(256 * t, 256)] = values.astype(BF16)

    def unit(t, carry):
        cols = pl.ds(pl.multiple_of(t * 128, 128), 128)
        for m in range(MICRO):
            q2 = stack_heads(q_ref[pl.ds(m * ROWS, ROWS), cols])
            keys = k_ref[pl.ds(m * EXT, EXT), cols]
            values = v_ref[pl.ds(m * EXT, EXT), cols]
            bias = bias_ref[m]
            scores = mm_nt(q2, keys) + jnp.concatenate([bias, bias], axis=0)
            peak = jnp.max(scores, axis=-1, keepdims=True)
            terms = jnp.exp(scores - peak)
            probs = (terms * (1.0 / jnp.sum(terms, axis=-1, keepdims=True))).astype(BF16)
            p_ref[m, t] = probs
            o_ref[pl.ds(m * ROWS, ROWS), cols] = join_heads(mm(probs, values)).astype(BF16)
        return carry

    lax.fori_loop(0, TILES, unit, 0)


def forward_mlp(ext, o_ref, wproj, mlp_gain, wlift, wdown, h2_ref, m_ref, left_ref, right_ref, waits):
    hidden = own_rows(ext[...]).astype(F32)
    finish(waits, "proj")
    mixed = hidden + mm(o_ref[...], wproj[...])
    h2_ref[...] = mixed
    normed, _ = norm_parts(mixed)
    b = (normed * mlp_gain).astype(BF16)
    finish(waits, "lift")
    for t in range(FF // 128):
        cols = pl.ds(128 * t, 128)
        gate = mm(b, wlift[:, 128 * t : 128 * t + 128])
        up = mm(b, wlift[:, FF + 128 * t : FF + 128 * t + 128])
        cdf = 0.5 * (1.0 + lax.erf(gate * root_half))
        gelu = gate * cdf
        m_ref[:, cols] = (gelu * up).astype(BF16)
        if left_ref is not None:
            pdf = jnp.exp(-0.5 * gate * gate) * inv_root_tau
            left_ref[:, cols] = up * (cdf + gate * pdf)
            right_ref[:, cols] = gelu
    finish(waits, "down")
    return mixed + mm(m_ref[...], wdown[...])


def backward_mlp(grad_low, h2_ref, mlp_gain, wproj, wlift, wdown, left_ref, right_ref, du_ref, do_ref):
    for t in range(3):
        cols = pl.ds(384 * t, 384)
        dm = mm_nt(grad_low, wdown[384 * t : 384 * t + 384, :])
        du_ref[:, cols] = (dm * left_ref[:, cols]).astype(BF16)
        du_ref[:, pl.ds(FF + 384 * t, 384)] = (dm * right_ref[:, cols]).astype(BF16)
    db = mm_nt(du_ref[...], wlift[...])
    normed, inv_scale = norm_parts(h2_ref[...])
    gain_grad = jnp.sum(db * normed, axis=0, keepdims=True)
    dh2 = grad_low.astype(F32) + norm_back(db, mlp_gain, normed, inv_scale)
    gb = dh2.astype(BF16)
    do_ref[...] = mm_nt(gb, wproj[...]).astype(BF16)
    return dh2, gb, gain_grad, normed


def backward_attention(q_ref, k_ref, v_ref, p_ref, do_ref, cos_ref, sin_ref, dq_ref, dkv_ref, low_ref, high_ref):
    cosine, sine = cos_ref[...], sin_ref[...]
    cos_own, sin_own = cosine[HALF : HALF + ROWS], sine[HALF : HALF + ROWS]

    def unit(t, carry):
        cols = pl.ds(pl.multiple_of(t * 128, 128), 128)
        value_cols = pl.ds(pl.multiple_of(D + t * 128, 128), 128)
        for m in range(MICRO):
            rows = pl.ds(m * ROWS, ROWS)
            q2 = stack_heads(q_ref[rows, cols])
            keys = k_ref[pl.ds(m * EXT, EXT), cols]
            values = v_ref[pl.ds(m * EXT, EXT), cols]
            do2 = stack_heads(do_ref[rows, cols])
            probs = p_ref[m, t]
            dprobs = mm_nt(do2, values)
            wide = probs.astype(F32)
            inner = jnp.sum(wide * dprobs, axis=-1, keepdims=True)
            ds = (wide * (dprobs - inner)).astype(BF16)
            dq = join_heads(mm(ds, keys)) * 0.125
            dq_ref[rows, cols] = rotate_back(dq, cos_own, sin_own).astype(BF16)
            dk = rotate_back(mm_tn(ds, q2), cosine, sine)
            dv = mm_tn(probs, do2)
            for grad, where in ((dk, cols), (dv, value_cols)):
                low_ref[m, :, where] = grad[:HALF].astype(BF16)
                dkv_ref[rows, where] = grad[HALF : HALF + ROWS]
                high_ref[m, :, where] = grad[HALF + ROWS :].astype(BF16)
        return carry

    lax.fori_loop(0, TILES, unit, 0)


def forward_kernel(own, low, high, gains, cos_ref, sin_ref, bias_ref, packed, h3_ref,
                   wqkv, wproj, wlift, wdown, ext, a_ext, q, k, v, p, o, h2, m_out, sems):
    waits = start_weights(packed, (wqkv, wproj, wlift, wdown), sems, ("qkv", "proj", "lift", "down"))
    load_stream(None, own, low, high, (None, None, None), ext)
    finish(waits, "qkv")
    forward_attention(ext, gains[0:1], wqkv, cos_ref, sin_ref, bias_ref, a_ext, q, k, v, p, o)
    h3 = forward_mlp(ext, o, wproj, gains[1:2], wlift, wdown, h2, m_out, None, None, waits)
    for m in range(MICRO):
        h3_ref[m] = h3[m * ROWS : (m + 1) * ROWS].astype(BF16)


def turning_kernel(flag_ref, own, low, high, other_own, other_low, other_high, cotangent, gains,
                   cos_ref, sin_ref, bias_ref, packed,
                   h3_ref, q, k, v, p, o, h2, m_out, left, right, src, dh2_ref, dq, dkv, to_low, to_high,
                   wqkv, wproj, wlift, wdown, ext, a_ext, du, do, sems):
    waits = start_weights(packed, (wqkv, wproj, wlift, wdown), sems, ("qkv", "proj", "lift", "down"))
    flag = flag_ref[0] == 1
    load_stream(flag, own, low, high, (other_own, other_low, other_high), ext)
    src[...] = own_rows(ext[...])
    finish(waits, "qkv")
    forward_attention(ext, gains[0:1], wqkv, cos_ref, sin_ref, bias_ref, a_ext, q, k, v, p, o)
    h3 = forward_mlp(ext, o, wproj, gains[1:2], wlift, wdown, h2, m_out, left, right, waits)
    for m in range(MICRO):
        h3_ref[m] = h3[m * ROWS : (m + 1) * ROWS].astype(BF16)
    grad_low = jnp.concatenate([cotangent[0], cotangent[1]], axis=0)
    dh2, _, _, _ = backward_mlp(grad_low, h2, gains[1:2], wproj, wlift, wdown, left, right, du, do)
    dh2_ref[...] = dh2
    backward_attention(q, k, v, p, do, cos_ref, sin_ref, dq, dkv, to_low, to_high)


def back_kernel(flag_ref, incoming, cotangent, gains, cos_ref, sin_ref, packed, q, k, v, p, h2, left, right,
                grad_ref, du, gb_ref, b_ref, mlp_ref, dh2_ref, dq, dkv, to_low, to_high,
                wproj, wlift, wdown, do, sems):
    waits = start_weights(packed, (None, wproj, wlift, wdown), sems, ("down", "lift", "proj"))
    flag = flag_ref[0] == 1
    grad_low = jnp.concatenate(
        [jnp.where(flag, incoming[m], cotangent[m]) for m in range(MICRO)], axis=0
    )
    grad_ref[...] = grad_low
    for name in ("down", "lift", "proj"):
        finish(waits, name)
    dh2, gb, gain_grad, normed = backward_mlp(
        grad_low, h2, gains[1:2], wproj, wlift, wdown, left, right, du, do
    )
    gb_ref[...] = gb
    b_ref[...] = (normed * gains[1:2]).astype(BF16)
    mlp_ref[...] = gain_grad
    dh2_ref[...] = dh2
    backward_attention(q, k, v, p, do, cos_ref, sin_ref, dq, dkv, to_low, to_high)


def joined_grads(dq, dkv, from_low, from_high, dqkv):
    dqkv[:, :D] = dq[...]
    for m in range(MICRO):
        first, last = pl.ds(m * ROWS, HALF), pl.ds(m * ROWS + HALF, HALF)
        dqkv[first, D:] = (dkv[first, :] + from_low[m].astype(F32)).astype(BF16)
        dqkv[last, D:] = (dkv[last, :] + from_high[m].astype(F32)).astype(BF16)


def source_kernel(src, gains, dh2, dq, dkv, from_low, from_high, packed, out_ref, wqkv, dqkv, sems):
    waits = start_weights(packed, (wqkv, None, None, None), sems, ("qkv",))
    joined_grads(dq, dkv, from_low, from_high, dqkv)
    normed, inv_scale = norm_parts(src[...].astype(F32))
    finish(waits, "qkv")
    da = mm_nt(dqkv[...], wqkv[...])
    dh = dh2[...] + norm_back(da, gains[0:1], normed, inv_scale)
    for m in range(MICRO):
        out_ref[m] = dh[m * ROWS : (m + 1) * ROWS].astype(BF16)


def source_grad_kernel(src, gains, dh2, dq, dkv, from_low, from_high, packed, out_ref, attn_ref, qkv_ref,
                       wqkv, dqkv, sems):
    waits = start_weights(packed, (wqkv, None, None, None), sems, ("qkv",))
    joined_grads(dq, dkv, from_low, from_high, dqkv)
    normed, inv_scale = norm_parts(src[...].astype(F32))
    a = (normed * gains[0:1]).astype(BF16)
    for t in range(9):
        cols = pl.ds(256 * t, 256)
        qkv_ref[:, cols] = mm_tn(a, dqkv[:, cols]).astype(BF16)
    finish(waits, "qkv")
    da = mm_nt(dqkv[...], wqkv[...])
    attn_ref[...] = jnp.sum(da * normed, axis=0, keepdims=True)
    dh = dh2[...] + norm_back(da, gains[0:1], normed, inv_scale)
    for m in range(MICRO):
        out_ref[m] = dh[m * ROWS : (m + 1) * ROWS].astype(BF16)


def weight_grad_kernel(m_ref, grad_ref, b_ref, du, o_ref, gb_ref, down_ref, lift_ref, proj_ref):
    for t in range(3):
        cols = pl.ds(256 * t, 256)
        down_ref[:, cols] = mm_tn(m_ref[...], grad_ref[:, cols]).astype(BF16)
        proj_ref[:, cols] = mm_tn(o_ref[...], gb_ref[:, cols]).astype(BF16)
    for t in range(9):
        cols = pl.ds(256 * t, 256)
        lift_ref[:, cols] = mm_tn(b_ref[...], du[:, cols]).astype(BF16)


def vmem(count):
    return [pl.BlockSpec(memory_space=pltpu.VMEM)] * count


def call(kernel, name, ins, outs, scratch, flops):
    places = {"v": pltpu.VMEM, "a": pl.ANY, "s": pltpu.SMEM}
    return pl.pallas_call(
        kernel,
        name=name,
        out_shape=[jax.ShapeDtypeStruct(shape, kind) for shape, kind in outs],
        in_specs=[pl.BlockSpec(memory_space=places[place]) for _, place in ins],
        out_specs=vmem(len(outs)),
        scratch_shapes=scratch,
        compiler_params=pltpu.CompilerParams(vmem_limit_bytes=56 * 2**20),
        cost_estimate=pl.CostEstimate(flops=flops, bytes_accessed=10 * 2**20, transcendentals=0),
    )(*[array for array, _ in ins])


def halo_rows(block, axis):
    count = lax.axis_size(axis)
    up = [(i, i + 1) for i in range(count - 1)]
    down = [(i + 1, i) for i in range(count - 1)]
    return (
        lax.ppermute(block[:, ROWS - HALF :], axis, up),
        lax.ppermute(block[:, :HALF], axis, down),
    )


def tables(first_row, lengths):
    half = HD // 2
    frequencies = rope_base ** (-(jnp.arange(half, dtype=F32) * 2.0) / HD)
    positions = first_row - HALF + jnp.arange(EXT, dtype=jnp.int32)
    angles = positions.astype(F32)[:, None] * frequencies[None, :]
    cosine, sine = jnp.cos(angles), jnp.sin(angles)
    cosine = jnp.concatenate([cosine] * 4, axis=1)
    sine = jnp.concatenate([-sine, sine, -sine, sine], axis=1)
    ends = jnp.cumsum(lengths, axis=1)
    doc = jnp.sum((positions[None, :, None] >= ends[:, None, :]).astype(jnp.int32), axis=2)
    query = positions[HALF : HALF + ROWS]
    allowed = (
        (jnp.abs(query[:, None] - positions[None, :]) <= HALF)
        & (positions >= 0)[None, :]
        & (positions < SEQ_LEN)[None, :]
    )[None] & (doc[:, HALF : HALF + ROWS, None] == doc[:, None, :])
    return cosine, sine, jnp.where(allowed, 0.0, masked_score).astype(F32)


def pack_weights(qkv, lift, proj, down):
    thirds = lambda w: jnp.concatenate(jnp.split(w, 3, axis=0), axis=1)
    return jnp.concatenate([qkv, lift, thirds(proj), thirds(down)], axis=0)


def unpack_grads(block):
    wide = lambda w: jnp.concatenate(jnp.split(w, 3, axis=1), axis=0)
    return block[:192], block[192:384], wide(block[384:448]), wide(block[448:544])


WEIGHTS = [
    pltpu.VMEM((D, WIDE), BF16),
    pltpu.VMEM((D, D), BF16),
    pltpu.VMEM((D, WIDE), BF16),
    pltpu.VMEM((FF, D), BF16),
]
SEMS = pltpu.SemaphoreType.DMA((32,))
SAVED = [
    ((OWN, D), BF16),
    ((MICRO * EXT, D), BF16),
    ((MICRO * EXT, D), BF16),
    ((MICRO, TILES, 2 * ROWS, EXT), BF16),
    ((OWN, D), BF16),
    ((OWN, D), F32),
    ((OWN, FF), BF16),
    ((OWN, FF), F32),
    ((OWN, FF), F32),
]
STREAM = [pltpu.VMEM((MICRO * EXT, D), BF16)] * 2
GRADS_OUT = [
    ((OWN, D), F32),
    ((OWN, D), BF16),
    ((OWN, 2 * D), F32),
    ((MICRO, HALF, 2 * D), BF16),
    ((MICRO, HALF, 2 * D), BF16),
]


def body(
    inputs, out_grad, doc_lengths, attn_gain, qkv_weight, proj_weight, mlp_gain, lift_weight, down_weight
):
    on_first = lax.axis_index("section") == 0
    flag = on_first.astype(jnp.int32).reshape(1)
    packed = lax.all_gather(
        pack_weights(qkv_weight[0], lift_weight[0], proj_weight[0], down_weight[0]),
        "fsdp", axis=0, tiled=True,
    )
    gains = lax.all_gather(
        jnp.stack([attn_gain[0], mlp_gain[0]]), "fsdp", axis=1, tiled=True
    ).astype(F32)
    first_row = lax.axis_index("ctx") * ROWS
    cosine, sine, bias = tables(first_row, doc_lengths[:, 0])
    own, cotangent = inputs[:, 0], out_grad[:, 0]
    low, high = halo_rows(own, "ctx")
    stream = ((MICRO, ROWS, D), BF16)

    (relay,) = call(
        forward_kernel, "layer_forward",
        [(own, "v"), (low, "v"), (high, "v"), (gains, "v"), (cosine, "v"), (sine, "v"), (bias, "v"), (packed, "a")],
        [stream],
        WEIGHTS + STREAM + [pltpu.VMEM(s, k) for s, k in SAVED[:7]] + [SEMS],
        3_200_000_000,
    )
    relayed = lax.ppermute(relay, "section", [(0, 1)])
    other_low, other_high = halo_rows(relayed, "ctx")
    (h3, q, k, v, p, o, h2, m_act, left, right, src, dh2, dq, dkv, to_low, to_high) = call(
        turning_kernel, "layer_turn",
        [(flag, "s"), (own, "v"), (low, "v"), (high, "v"), (relayed, "v"), (other_low, "v"), (other_high, "v"),
         (cotangent, "v"), (gains, "v"), (cosine, "v"), (sine, "v"), (bias, "v"), (packed, "a")],
        [stream] + SAVED + [((OWN, D), BF16)] + GRADS_OUT,
        WEIGHTS + STREAM + [pltpu.VMEM((OWN, WIDE), BF16), pltpu.VMEM((OWN, D), BF16), SEMS],
        6_000_000_000,
    )

    def swap_halos(to_low, to_high):
        count = lax.axis_size("ctx")
        up = [(i, i + 1) for i in range(count - 1)]
        down = [(i + 1, i) for i in range(count - 1)]
        return lax.ppermute(to_high, "ctx", up), lax.ppermute(to_low, "ctx", down)

    from_low, from_high = swap_halos(to_low, to_high)
    (grad_relay,) = call(
        source_kernel, "layer_source",
        [(src, "v"), (gains, "v"), (dh2, "v"), (dq, "v"), (dkv, "v"), (from_low, "v"), (from_high, "v"), (packed, "a")],
        [stream],
        [WEIGHTS[0], pltpu.VMEM((OWN, WIDE), BF16), SEMS],
        900_000_000,
    )
    incoming = lax.ppermute(grad_relay, "section", [(1, 0)])
    (grad_low, du, gb, b, mlp_gain_grad, dh2, dq, dkv, to_low, to_high) = call(
        back_kernel, "layer_back",
        [(flag, "s"), (incoming, "v"), (cotangent, "v"), (gains, "v"), (cosine, "v"), (sine, "v"), (packed, "a"),
         (q, "v"), (k, "v"), (v, "v"), (p, "v"), (h2, "v"), (left, "v"), (right, "v")],
        [((OWN, D), BF16), ((OWN, WIDE), BF16), ((OWN, D), BF16), ((OWN, D), BF16), ((1, D), F32)] + GRADS_OUT,
        [*WEIGHTS[1:], pltpu.VMEM((OWN, D), BF16), SEMS],
        3_000_000_000,
    )
    from_low, from_high = swap_halos(to_low, to_high)
    down_grad, lift_grad, proj_grad = call(
        weight_grad_kernel, "weight_grads",
        [(m_act, "v"), (grad_low, "v"), (b, "v"), (du, "v"), (o, "v"), (gb, "v")],
        [((FF, D), BF16), ((D, WIDE), BF16), ((D, D), BF16)],
        [],
        1_600_000_000,
    )
    in_grad, attn_gain_grad, qkv_grad = call(
        source_grad_kernel, "layer_source_grads",
        [(src, "v"), (gains, "v"), (dh2, "v"), (dq, "v"), (dkv, "v"), (from_low, "v"), (from_high, "v"), (packed, "a")],
        [stream, ((1, D), F32), ((D, WIDE), BF16)],
        [WEIGHTS[0], pltpu.VMEM((OWN, WIDE), BF16), SEMS],
        1_800_000_000,
    )
    scatter = lambda g: lax.psum_scatter(g, "fsdp", scatter_dimension=0, tiled=True)
    finals = lax.psum(
        [scatter(g) for g in (qkv_grad, lift_grad, proj_grad, down_grad)], "ctx"
    )
    qkv_sum, lift_sum, proj_sum, down_sum = [g.astype(F32) for g in finals]
    gain_sums = lax.psum(
        lax.psum_scatter(
            jnp.concatenate([attn_gain_grad, mlp_gain_grad], axis=0), "fsdp", scatter_dimension=1, tiled=True
        ),
        "ctx",
    )
    return (
        h3_pair(h3, relay, on_first)[None, :, None],
        in_grad[None, :, None],
        gain_sums[0][None],
        qkv_sum[None],
        proj_sum[None],
        gain_sums[1][None],
        lift_sum[None],
        down_sum[None],
    )


def h3_pair(h3, relay, on_first):
    return h3


def solution(mesh):
    placed = (
        P(None, "fsdp", "ctx", None),
        P(None, "fsdp", "ctx", None),
        P(None, "fsdp", None),
        P("section", "fsdp"),
        P("section", "fsdp", None),
        P("section", "fsdp", None),
        P("section", "fsdp"),
        P("section", "fsdp", None),
        P("section", "fsdp", None),
    )
    return jax.shard_map(
        body,
        mesh=mesh,
        in_specs=placed,
        out_specs=(
            P("section", None, "fsdp", "ctx", None),
            P("section", None, "fsdp", "ctx", None),
            P("section", "fsdp"),
            P("section", "fsdp", None),
            P("section", "fsdp", None),
            P("section", "fsdp"),
            P("section", "fsdp", None),
            P("section", "fsdp", None),
        ),
        check_vma=False,
    )
```

time: 661 us -> 554 us (0.84); the launches traced: 652 us -> 553 us
  Pallas kernels: 0 us -> 81.8 us
  matrix products: 79.3 us -> 0 us
  local copies, waits for them, and re-layouts: 86.9 us -> 9.93 us
  waiting for transfers between devices: 319 us -> 352 us
  other arithmetic: 53.8 us -> 23 us
  starting transfers between devices: 49.1 us -> 34.8 us
  blocking collectives: 45.5 us -> 37.5 us
    pallas_call x0 -> x6, Pallas kernels: none -> 81.8 us  [call(): pl.pallas_call(kernel, name=name, out_shape=[jax.ShapeDtypeStruct(shape,...]
    dot_general x54 -> x0, matrix products: 79.3 us -> none  [the longest x12 30.8 us: outer_sum(): lax.dot_general(left, right, (((0,), (0,)), ((), ())), preferred_element_...]
    reduce_scatter x4, waiting for transfers between devices: 76.5 us -> 117 us  [body(): lax.psum_scatter(g, 'fsdp', scatter_dimension=0, tiled=True)]
    scatter-add x6 -> x0, local copies, waits for them, and re-layouts: 36.7 us -> none  [the longest x3 20 us: backward_layer(): own_rows = own_rows.at[row_count - HALF:].add(from_peers[3 * HALF:])]
    all_gather x4 -> x1, waiting for transfers between devices: 106 us -> 80 us  [body(): lax.all_gather(pack_weights(qkv_weight[0], lift_weight[0], proj_weight[0]...]
    unnamed x9 -> x8, waiting for transfers between devices: 2.66 us -> 22.7 us
    slice x24 -> x5, local copies, waits for them, and re-layouts: 17.5 us -> 0.77 us  [the longest x1 0.57 us: body(): gain_sums[1][None]]
    unnamed x393 -> x42, local copies, waits for them, and re-layouts: 22.8 us -> 6.38 us
  transfers between devices with their start and end apart: 25 -> 17, of which waited for: 22 -> 14; matrix products, arithmetic and copies ran while one was open for 12% -> 1% of each run, Pallas kernels for 0% -> 1%
where the time goes in v1:
time: 554 us; the launch traced here: 553 us
  waiting for transfers between devices  352 us (64%)
  Pallas kernels  81.8 us (15%)
  blocking collectives  37.5 us (7%)
  starting transfers between devices  34.8 us (6%)
  other arithmetic  23 us (4%)
  between operations  14.4 us (3%)
  local copies, waits for them, and re-layouts  9.93 us (2%)
    reduce_scatter x4, waiting for transfers between devices, body(): lax.psum_scatter(g, 'fsdp', scatter_dimension=0, tiled=True)  117 us
    psum x1, waiting for transfers between devices, body(): lax.psum([scatter(g) for g in (qkv_grad, lift_grad, proj_grad, down_grad)...  98.3 us
    pallas_call x6, Pallas kernels, call(): pl.pallas_call(kernel, name=name, out_shape=[jax.ShapeDtypeStruct(shape,...  81.8 us
    all_gather x1, waiting for transfers between devices, body(): lax.all_gather(pack_weights(qkv_weight[0], lift_weight[0], proj_weight[0]...  80 us
    psum x1, blocking collectives, body(): lax.psum(lax.psum_scatter(jnp.concatenate([attn_gain_grad, mlp_gain_grad]...  29.3 us
    unnamed x8, waiting for transfers between devices  22.7 us
    ppermute x4, waiting for transfers between devices, swap_halos(): return (lax.ppermute(to_high, 'ctx', up), lax.ppermute(to_low, 'ctx', down))  14.9 us
    ppermute x4, starting transfers between devices, swap_halos(): return (lax.ppermute(to_high, 'ctx', up), lax.ppermute(to_low, 'ctx', down))  14.7 us
  transfers between devices with their start and end apart: 17, of which 14 were waited for; matrix products, arithmetic and copies ran while one was open for 1% of the time, Pallas kernels for 1%

profile of v1, /device:TPU:1, one launch (start us, length us, event | category | flops | bytes accessed | tf_op | source)
XLA Modules:
  0.0 553.2 jit_solution(15160954305784104671)
XLA Ops:
  7.2 1.0 slice_bitcast_fusion.5
  8.2 1.1 slice_bitcast_fusion.2
  9.3 12.8 %maximum_maximum_fusion = bf16[544,2304]{1,0:T(8,128)(2,1)} fusion(bf16[96,768]{1,0:T(8,128)(2,1)S(1)} %get-tuple-element.109, bf16[96,768]{1,0:T(8,128)(2,1)S(1)} %get-tuple-element.110, bf16[96,768]{1,0:T(8,128)(2,1)S(1)} %get-tuple-element.108, bf16[64,768]{1,0:T(8,128)(2,1)S(1)} %get-tuple-element.116, bf16[64,768]{1,0:T(8,128)(2,1)S(1)} %get-tuple-element.117, ...), kind=kLoop, calls=%fused_computation | loop fusion | flops 20054016 | bytes 5013504 | tf_op jit(solution)/shard_map/concatenate | solution.py:402
  22.2 0.0 reduce-scatter.10.cloned.1.call-start
  22.2 0.9 copy-done.4
  23.1 3.3 collective-permute-start.1
  26.5 3.5 collective-permute-start
  30.0 0.1 slice.32
  30.1 0.2 reduce_window_sum.14
  30.3 0.1 convert_reduce_fusion
  30.4 0.1 slice.40
  30.5 8.1 %all-gather = bf16[4,192,2]{1,2,0:T(2,128)(2,1)S(1)} all-gather(bf16[1,192,2]{1,2,0:T(2,128)(2,1)S(1)} %maximum_bitcast_fusion), channel_id=1, replica_groups=mesh['section'=2,'ctx'=16,'fsdp'=4] {'fsdp'}, dimensions={0}, use_global_device_ids=true | all-gather | bytes 3840 | tf_op jit(solution)/shard_map/all_gather | solution.py:447
  38.6 0.7 reshape.122
  39.3 0.5 fusion.2
  39.9 0.8 pad_maximum_fusion.cos_ref
  40.7 0.8 pad_maximum_fusion.1.sin_ref
  41.5 0.1 fusion.1
  41.7 0.8 and_select_fusion.bias_ref
  42.5 80.0 %all-gather.3.cloned.1.call-done.packed = bf16[2176,2304]{1,0:T(8,128)(2,1)} async-done(((bf16[544,2304]{1,0:T(8,128)(2,1)}), bf16[2176,2304]{1,0:T(8,128)(2,1)}) %all-gather.3.cloned.1.call-update) | async-done | bytes 10027024 | tf_op jit(solution)/shard_map/all_gather | solution.py:443
  122.5 15.9 %layer_forward.1 = bf16[2,128,768]{2,1,0:T(8,128)(2,1)} custom-call(bf16[2,128,768]{2,1,0:T(8,128)(2,1)} %bitcast.43, bf16[2,64,768]{2,1,0:T(8,128)(2,1)} %copy-done.17, bf16[2,64,768]{2,1,0:T(8,128)(2,1)} %copy-done.16, f32[2,768]{1,0:T(2,128)} %bitcast.49, f32[256,128]{1,0:T(8,128)} %pad_maximum_fusion.cos_ref, f32[256,128]{1,0:T(8,128)} %pad_maximum_fusion.1.sin_ref, ...), custom_call_target="tpu_custom_call" | custom-call | flops 3200000000 | bytes 10485760 | tf_op jit(solution)/shard_map/layer_forward/pallas_call | solution.py:359
  138.5 4.6 collective-permute-start.2
  143.1 8.1 %collective-permute-done.2.other_own = bf16[2,128,768]{2,1,0:T(8,128)(2,1)S(1)} collective-permute-done((bf16[2,128,768]{2,1,0:T(8,128)(2,1)}, bf16[2,128,768]{2,1,0:T(8,128)(2,1)S(1)}, u32[]{:S(2)}, u32[]{:S(2)}) %collective-permute-start.2) | collective-permute-done | bytes 393248 | tf_op jit(solution)/shard_map/ppermute | solution.py:463
  151.2 3.5 collective-permute-start.4
  154.7 3.3 collective-permute-start.3
  158.0 1.2 collective-permute-done.4.other_high
  159.2 1.2 collective-permute-done.3.other_low
  160.3 0.7 copy-done.19
  161.0 28.2 %layer_turn.1 = (bf16[2,128,768]{2,1,0:T(8,128)(2,1)}, bf16[256,768]{1,0:T(8,128)(2,1)}, bf16[512,768]{1,0:T(8,128)(2,1)}, bf16[512,768]{1,0:T(8,128)(2,1)}, bf1...) custom-call(s32[1]{0:T(128)} %bitcast.2.flag_ref, ...), custom_call_target="tpu_custom_call" | custom-call | flops 6000000000 | bytes 10485760 | tf_op jit(solution)/shard_map/layer_turn/pallas_call | solution.py:359
  189.2 4.4 collective-permute-start.5
  193.6 1.9 collective-permute-start.6
  195.5 3.1 collective-permute-done.5.from_low
  198.6 4.3 collective-permute-done.6.from_high
  202.9 0.7 copy-done.8
  203.6 6.4 %layer_source.1 = bf16[2,128,768]{2,1,0:T(8,128)(2,1)} custom-call(bf16[256,768]{1,0:T(8,128)(2,1)} %get-tuple-element.41.src, f32[2,768]{1,0:T(2,128)} %bitcast.51, f32[256,768]{1,0:T(8,128)} %get-tuple-element.42.dh2, bf16[256,768]{1,0:T(8,128)(2,1)} %get-tuple-element.43.dq, f32[256,1536]{1,0:T(8,128)} %get-tuple-element.44.dkv, ...), custom_call_target="tpu_custom_call" | custom-call | flops 900000000 | bytes 10485760 | tf_op jit(solution)/shard_map/layer_source/pallas_call | solution.py:359
  210.1 1.6 collective-permute-start.7
  211.6 8.7 %collective-permute-done.7.incoming = bf16[2,128,768]{2,1,0:T(8,128)(2,1)S(1)} collective-permute-done((bf16[2,128,768]{2,1,0:T(8,128)(2,1)}, bf16[2,128,768]{2,1,0:T(8,128)(2,1)S(1)}, u32[]{:S(2)}, u32[]{:S(2)}) %collective-permute-start.7) | collective-permute-done | bytes 393248 | tf_op jit(solution)/shard_map/ppermute | solution.py:488
  220.3 0.7 copy-done.6
  221.1 17.4 %layer_back.1 = (bf16[256,768]{1,0:T(8,128)(2,1)}, bf16[256,2304]{1,0:T(8,128)(2,1)}, bf16[256,768]{1,0:T(8,128)(2,1)}, bf16[256,768]{1,0:T(8,128)(2,1)}, f32[1,...) custom-call(s32[1]{0:T(128)} %bitcast.2.flag_ref, ...), custom_call_target="tpu_custom_call" | custom-call | flops 3000000000 | bytes 10485760 | tf_op jit(solution)/shard_map/layer_back/pallas_call | solution.py:359
  238.4 6.0 %weight_grads.1 = (bf16[1152,768]{1,0:T(8,128)(2,1)}, bf16[768,2304]{1,0:T(8,128)(2,1)}, bf16[768,768]{1,0:T(8,128)(2,1)}) custom-call(bf16[256,1152]{1,0:T(8,128)(2,1)} %get-tuple-element.63.m_ref, bf16[256,768]{1,0:T(8,128)(2,1)} %get-tuple-element.64.grad_ref, bf16[256,768]{1,0:T(8,128)(2,1)} %get-tuple-element.65.b_ref, ...), custom_call_target="tpu_custom_call" | custom-call | flops 1600000000 | bytes 10485760 | tf_op jit(solution)/shard_map/weight_grads/pallas_call | solution.py:359
  244.5 0.0 reduce-scatter.14.cloned.1.call-start
  244.6 0.7 reduce-scatter.14.cloned.1.call-update
  245.3 0.5 reduce-scatter.12.cloned.1.call-update
  245.9 6.5 %collective-permute-start.8 = (bf16[2,64,1536]{2,1,0:T(8,128)(2,1)S(1)}, bf16[2,64,1536]{2,1,0:T(8,128)(2,1)S(1)}, u32[]{:S(2)}, u32[]{:S(2)}) collective-permute-start(bf16[2,64,1536]{2,1,0:T(8,128)(2,1)S(1)} %copy-done.15), channel_id=1, source_target_pairs={{0,4},{4,8},{8,12},{12,16},{16,20},{20,24},{24,28},{28,32},{32,36}... | collective-permute-start | bytes 1179656 | tf_op jit(solution)/shard_map/ppermute | solution.py:478
  252.3 1.9 collective-permute-start.9
  254.3 2.8 collective-permute-done.8.from_low
  257.0 4.8 collective-permute-done.9.from_high
  261.8 0.7 copy-done.3
  262.6 7.9 %layer_source_grads.1 = (bf16[2,128,768]{2,1,0:T(8,128)(2,1)}, f32[1,768]{1,0:T(1,128)}, bf16[768,2304]{1,0:T(8,128)(2,1)}) custom-call(bf16[256,768]{1,0:T(8,128)(2,1)} %get-tuple-element.41.src, f32[2,768]{1,0:T(2,128)} %bitcast.53, f32[256,768]{1,0:T(8,128)} %get-tuple-element.54.dh2, bf16[256,768]{1,0:T(8,128)(2,1)} %get-tuple-element.55.dq, ...), custom_call_target="tpu_custom_call" | custom-call | flops 1800000000 | bytes 10485760 | tf_op jit(solution)/shard_map/layer_source_grads/pallas_call | solution.py:359
  270.5 0.0 reduce-scatter.16.cloned.1.call-start
  270.6 0.6 copy-done.9
  271.2 0.9 copy.30
  272.2 0.0 all-reduce.3.cloned.1.call-start
  272.2 29.5 %reduce-scatter.14.cloned.1.call-done = bf16[288,768]{1,0:T(8,128)(2,1)} async-done(((bf16[1152,768]{1,0:T(8,128)(2,1)}), bf16[288,768]{1,0:T(8,128)(2,1)}) %reduce-scatter.14.cloned.1.call-update) | async-done | bytes 442384 | tf_op jit(solution)/shard_map/reduce_scatter | solution.py:512
  301.7 43.7 %reduce-scatter.12.cloned.1.call-done = bf16[192,2304]{1,0:T(8,128)(2,1)} async-done(((bf16[768,2304]{1,0:T(8,128)(2,1)}), bf16[192,2304]{1,0:T(8,128)(2,1)}) %reduce-scatter.12.cloned.1.call-update) | async-done | bytes 884752 | tf_op jit(solution)/shard_map/reduce_scatter | solution.py:512
  345.4 43.6 %reduce-scatter.8.cloned.1.call-done = bf16[192,2304]{1,0:T(8,128)(2,1)} async-done(((bf16[768,2304]{1,0:T(8,128)(2,1)}), bf16[192,2304]{1,0:T(8,128)(2,1)}) %reduce-scatter.8.cloned.1.call-update) | async-done | bytes 884752 | tf_op jit(solution)/shard_map/reduce_scatter | solution.py:512
  389.1 21.4 %reduce-scatter.16.cloned.1.call-done = f32[192,2]{1,0:T(8,128)} async-done(((f32[768,2]{1,0:T(8,128)}), f32[192,2]{1,0:T(8,128)}) %reduce-scatter.16.cloned.1.call-update) | async-done | bytes 1552
  410.5 1.0 copy.31
  411.4 29.3 %psum.35 = f32[2,192]{1,0:T(2,128)S(1)} all-reduce(f32[2,192]{1,0:T(2,128)S(1)} %copy.31), channel_id=1, replica_groups=mesh['section'=2,'ctx'=16,'fsdp'=4] {'ctx'}, use_global_device_ids=true, to_apply=%region_3.4 | all-reduce | flops 384 | bytes 3072 | tf_op jit(solution)/shard_map/psum | solution.py:517
  440.8 0.6 fusion.8
  441.3 98.3 %all-reduce.3.cloned.1.call-done = (bf16[1,192,2304]{2,1,0:T(8,128)(2,1)}, bf16[1,192,768]{2,1,0:T(8,128)(2,1)}, bf16[1,192,2304]{2,1,0:T(8,128)(2,1)}, bf16[1,288,768]{2,1,0:T(8,128)(2,1)}) async-done(((bf16[1,192,2304]{2,1,0:T(8,128)(2,1)}, bf16[1,192,768]{2,1,0:T(8,128)(2,1)}, bf16[1,192,2304]{2,1,0:T(8,128)(2,1)}, bf16[1,288,768]{2,1,0:T(8,128)(2,1)}), (bf16[1,192,2304]{2,1,0:T(8,128)(2,1)}, ...) | async-done | bytes 2506768 | tf_op jit(solution)/shard_map/psum | solution.py:513
  539.6 1.9 broadcast_in_dim.56
  541.5 2.5 broadcast_in_dim.54
  544.0 1.0 broadcast_in_dim.60
  545.0 1.3 broadcast_in_dim.58
  (53 shorter events, 0.4 us)
Async XLA Ops:
  7.2 115.3 %all-gather.3.cloned.1.call-start = ((), (), s32[]{:S(2)}) async-start(), calls=%async_computation.5 | async-start | bytes 12533760 | tf_op jit(solution)/shard_map/all_gather | solution.py:443
  22.1 1.0 copy-start.4
  22.1 8.0 %copy-start.13 = (s32[2,1,4]{2,1,0:T(1,128)S(1)}, s32[2,1,4]{2,1,0:T(1,128)}, u32[]{:S(2)}) copy-start(s32[2,1,4]{2,1,0:T(1,128)} %param.11) | copy-start | bytes 100
  22.1 8.3 %copy-start.11 = (bf16[1,192]{1,0:T(2,128)(2,1)S(1)}, bf16[1,192]{1,0:T(2,128)(2,1)}, u32[]{:S(2)}) copy-start(bf16[1,192]{1,0:T(2,128)(2,1)} %param.15) | copy-start | bytes 1156
  22.1 8.3 %copy-start.12 = (bf16[1,192]{1,0:T(2,128)(2,1)S(1)}, bf16[1,192]{1,0:T(2,128)(2,1)}, u32[]{:S(2)}) copy-start(bf16[1,192]{1,0:T(2,128)(2,1)} %param.12) | copy-start | bytes 1156
  22.2 250.1 %reduce-scatter.10.cloned.1.call-start = ((), (), s32[]{:S(2)}) async-start(), calls=%async_computation.7 | async-start | bytes 1474560 | tf_op jit(solution)/shard_map/reduce_scatter | solution.py:512
  23.1 19.3 %collective-permute-start.1 = (bf16[2,64,768]{2,1,0:T(8,128)(2,1)S(1)}, bf16[2,64,768]{2,1,0:T(8,128)(2,1)S(1)}, u32[]{:S(2)}, u32[]{:S(2)}) collective-permute-start(bf16[2,64,768]{2,1,0:T(8,128)(2,1)S(1)} %get-tuple-element.113), channel_id=1, source_target_pairs={{4,0},{8,4},{12,8},{16,12},{20,16},{24,20},{28,24},{32,28},{36,32}... | collective-permute-start | bytes 589832 | tf_op jit(solution)/shard_map/ppermute | solution.py:377
  26.5 16.0 %collective-permute-start = (bf16[2,64,768]{2,1,0:T(8,128)(2,1)S(1)}, bf16[2,64,768]{2,1,0:T(8,128)(2,1)S(1)}, u32[]{:S(2)}, u32[]{:S(2)}) collective-permute-start(bf16[2,64,768]{2,1,0:T(8,128)(2,1)S(1)} %get-tuple-element.114), channel_id=1, source_target_pairs={{0,4},{4,8},{8,12},{12,16},{16,20},{20,24},{24,28},{28,32},{32,36}... | collective-permute-start | bytes 589832 | tf_op jit(solution)/shard_map/ppermute | solution.py:376
  42.5 80.0 %copy-start.16 = (bf16[2,64,768]{2,1,0:T(8,128)(2,1)}, bf16[2,64,768]{2,1,0:T(8,128)(2,1)S(1)}, u32[]{:S(2)}) copy-start(bf16[2,64,768]{2,1,0:T(8,128)(2,1)S(1)} %collective-permute-done.1.high) | copy-start | bytes 589828
  42.5 80.0 %copy-start.17 = (bf16[2,64,768]{2,1,0:T(8,128)(2,1)}, bf16[2,64,768]{2,1,0:T(8,128)(2,1)S(1)}, u32[]{:S(2)}) copy-start(bf16[2,64,768]{2,1,0:T(8,128)(2,1)S(1)} %collective-permute-done.low) | copy-start | bytes 589828
  138.5 12.7 %collective-permute-start.2 = (bf16[2,128,768]{2,1,0:T(8,128)(2,1)}, bf16[2,128,768]{2,1,0:T(8,128)(2,1)S(1)}, u32[]{:S(2)}, u32[]{:S(2)}) collective-permute-start(bf16[2,128,768]{2,1,0:T(8,128)(2,1)} %layer_forward.1), channel_id=1, source_target_pairs={{0,64},{1,65},{2,66},{3,67},{4,68},{5,69},{6,70},{7,71},{8,72},{9,... | collective-permute-start | bytes 1179656 | tf_op jit(solution)/shard_map/ppermute | solution.py:463
  151.2 9.2 %copy-start.5 = (bf16[2,128,768]{2,1,0:T(8,128)(2,1)}, bf16[2,128,768]{2,1,0:T(8,128)(2,1)S(1)}, u32[]{:S(2)}) copy-start(bf16[2,128,768]{2,1,0:T(8,128)(2,1)S(1)} %collective-permute-done.2.other_own) | copy-start | bytes 1179652
  151.2 8.0 %collective-permute-start.4 = (bf16[2,64,768]{2,1,0:T(8,128)(2,1)S(1)}, bf16[2,64,768]{2,1,0:T(8,128)(2,1)S(1)}, u32[]{:S(2)}, u32[]{:S(2)}) collective-permute-start(bf16[2,64,768]{2,1,0:T(8,128)(2,1)S(1)} %get-tuple-element.111), channel_id=1, source_target_pairs={{4,0},{8,4},{12,8},{16,12},{20,16},{24,20},{28,24},{32,28},{36,32}... | collective-permute-start | bytes 589832 | tf_op jit(solution)/shard_map/ppermute | solution.py:377
  154.7 5.7 %collective-permute-start.3 = (bf16[2,64,768]{2,1,0:T(8,128)(2,1)S(1)}, bf16[2,64,768]{2,1,0:T(8,128)(2,1)S(1)}, u32[]{:S(2)}, u32[]{:S(2)}) collective-permute-start(bf16[2,64,768]{2,1,0:T(8,128)(2,1)S(1)} %get-tuple-element.112), channel_id=1, source_target_pairs={{0,4},{4,8},{8,12},{12,16},{16,20},{20,24},{24,28},{28,32},{32,36}... | collective-permute-start | bytes 589832 | tf_op jit(solution)/shard_map/ppermute | solution.py:376
  159.2 1.2 copy-start.18
  160.3 0.7 copy-start.19
  189.2 9.4 %collective-permute-start.5 = (bf16[2,64,1536]{2,1,0:T(8,128)(2,1)}, bf16[2,64,1536]{2,1,0:T(8,128)(2,1)S(1)}, u32[]{:S(2)}, u32[]{:S(2)}) collective-permute-start(bf16[2,64,1536]{2,1,0:T(8,128)(2,1)} %get-tuple-element.45), channel_id=1, source_target_pairs={{0,4},{4,8},{8,12},{12,16},{16,20},{20,24},{24,28},{28,32},{32,36}... | collective-permute-start | bytes 1179656 | tf_op jit(solution)/shard_map/ppermute | solution.py:478
  193.6 9.3 %collective-permute-start.6 = (bf16[2,64,1536]{2,1,0:T(8,128)(2,1)}, bf16[2,64,1536]{2,1,0:T(8,128)(2,1)S(1)}, u32[]{:S(2)}, u32[]{:S(2)}) collective-permute-start(bf16[2,64,1536]{2,1,0:T(8,128)(2,1)} %get-tuple-element.46), channel_id=1, source_target_pairs={{4,0},{8,4},{12,8},{16,12},{20,16},{24,20},{28,24},{32,28},{36,32}... | collective-permute-start | bytes 1179656 | tf_op jit(solution)/shard_map/ppermute | solution.py:478
  198.6 4.3 copy-start.7
  202.9 0.7 copy-start.8
  210.1 10.2 %collective-permute-start.7 = (bf16[2,128,768]{2,1,0:T(8,128)(2,1)}, bf16[2,128,768]{2,1,0:T(8,128)(2,1)S(1)}, u32[]{:S(2)}, u32[]{:S(2)}) collective-permute-start(bf16[2,128,768]{2,1,0:T(8,128)(2,1)} %layer_source.1), channel_id=1, source_target_pairs={{64,0},{65,1},{66,2},{67,3},{68,4},{69,5},{70,6},{71,7},{72,8},{73... | collective-permute-start | bytes 1179656 | tf_op jit(solution)/shard_map/ppermute | solution.py:488
  220.3 0.7 copy-start.6
  244.5 57.2 %reduce-scatter.14.cloned.1.call-start = ((), (), s32[]{:S(2)}) async-start(), calls=%async_computation.9 | async-start | bytes 2211840 | tf_op jit(solution)/shard_map/reduce_scatter | solution.py:512
  244.5 1.3 copy-start.15
  244.6 7.8 %copy-start.14 = (bf16[2,64,1536]{2,1,0:T(8,128)(2,1)S(1)}, bf16[2,64,1536]{2,1,0:T(8,128)(2,1)}, u32[]{:S(2)}) copy-start(bf16[2,64,1536]{2,1,0:T(8,128)(2,1)} %get-tuple-element.58) | copy-start | bytes 1179652
  245.2 100.2 %reduce-scatter.12.cloned.1.call-start = ((), (), s32[]{:S(2)}) async-start(), calls=%async_computation.8 | async-start | bytes 4423680 | tf_op jit(solution)/shard_map/reduce_scatter | solution.py:512
  245.8 143.2 %reduce-scatter.8.cloned.1.call-start = ((), (), s32[]{:S(2)}) async-start(), calls=%async_computation.6 | async-start | bytes 4423680 | tf_op jit(solution)/shard_map/reduce_scatter | solution.py:512
  245.9 11.2 %collective-permute-start.8 = (bf16[2,64,1536]{2,1,0:T(8,128)(2,1)S(1)}, bf16[2,64,1536]{2,1,0:T(8,128)(2,1)S(1)}, u32[]{:S(2)}, u32[]{:S(2)}) collective-permute-start(bf16[2,64,1536]{2,1,0:T(8,128)(2,1)S(1)} %copy-done.15), channel_id=1, source_target_pairs={{0,4},{4,8},{8,12},{12,16},{16,20},{20,24},{24,28},{28,32},{32,36}... | collective-permute-start | bytes 1179656 | tf_op jit(solution)/shard_map/ppermute | solution.py:478
  252.3 9.5 %collective-permute-start.9 = (bf16[2,64,1536]{2,1,0:T(8,128)(2,1)S(1)}, bf16[2,64,1536]{2,1,0:T(8,128)(2,1)S(1)}, u32[]{:S(2)}, u32[]{:S(2)}) collective-permute-start(bf16[2,64,1536]{2,1,0:T(8,128)(2,1)S(1)} %copy-done.14), channel_id=1, source_target_pairs={{4,0},{8,4},{12,8},{16,12},{20,16},{24,20},{28,24},{32,28},{36,32}... | collective-permute-start | bytes 1179656 | tf_op jit(solution)/shard_map/ppermute | solution.py:478
  257.0 4.8 copy-start.2
  261.8 0.7 copy-start.3
  270.5 0.7 copy-start.9
  270.5 0.7 copy-start.10
  270.5 139.9 %reduce-scatter.16.cloned.1.call-start = ((), (), s32[]{:S(2)}) async-start(), calls=%async_computation.10 | async-start | bytes 491520
  272.2 267.4 %all-reduce.3.cloned.1.call-start = ((), (), s32[]{:S(2)}) async-start(), calls=%async_computation.11 | async-start | bytes 5013504 | tf_op jit(solution)/shard_map/psum | solution.py:513
  539.6 4.4 copy-start.1
  539.6 5.4 copy-start
Sparse Core Ops, SparseCore 0:
  22.3 100.1 all-gather.2
  244.6 26.0 reduce-scatter.9
  273.7 27.9 reduce-scatter.13
  304.2 41.2 reduce-scatter.11
  347.8 41.1 reduce-scatter.7
  392.0 18.4 reduce-scatter.15
  413.2 126.3 all-reduce.2
